TPU v7x, 256 devices: a whole 4x4x8 slice. The times are simulated.
256 devices in a mesh: src: 32 (over y, x, core), tgt: 8 (over z).
Axes of the slice: x: 4, y: 4, z: 8, core: 2. Of those that a mesh axis runs over, the one named last changes fastest.
Arguments:
- sources: float32 [32768, 128], P(('src', 'tgt')), may hold values from -4 to 4
- targets: float32 [65536, 128], P(('tgt', 'src')), may hold values from -4 to 4
- potential_in: float32 [65536], P('tgt'), may hold values from -1 to 1
Outputs:
- source_potential: float32 [32768], P('src')
- target_potential: float32 [65536], P('tgt')
- mapped: float32 [32768, 128], P(('src', 'tgt'))
All inputs are finite; a program needn't handle non-finite values.
Results may differ from a plain program's by a relative error of at most 0.0003.
Values sent between devices are 32-bit elements; how exact they have to be, the bound alone decides.
A program may use at most 128 MiB of HBM per device.

v0:
```python
import math

import jax
import jax.numpy as jnp
from jax import lax
from jax.sharding import PartitionSpec as P

epsilon = 0.05


def joined(array, axis, combine):
    everything = jax.tree.map(lambda part: lax.all_gather(part, axis), array)
    first = jax.tree.map(lambda part: part[0], everything)

    def step(k, so_far):
        return combine(so_far, jax.tree.map(lambda part: part[k], everything))

    return lax.fori_loop(1, lax.axis_size(axis), step, first)


def lse_combine(first, second):
    top = jnp.maximum(first[0], second[0])
    return (top, first[1] * jnp.exp(first[0] - top) + second[1] * jnp.exp(second[0] - top))


def map_combine(first, second):
    top = jnp.maximum(first[0], second[0])
    scale_one = jnp.exp(first[0] - top)
    scale_two = jnp.exp(second[0] - top)
    return (
        top,
        first[1] * scale_one + second[1] * scale_two,
        first[2] * scale_one[:, None] + second[2] * scale_two[:, None],
    )


def per_device(sources, targets, potential_in):
    src_rows = lax.all_gather(sources, "tgt", axis=0, tiled=True)
    tgt_rows = lax.all_gather(targets, "src", axis=0, tiled=True)
    local_src = src_rows.shape[0]
    local_tgt = tgt_rows.shape[0]
    width = src_rows.shape[1]
    num_src = local_src * lax.axis_size("src")
    num_tgt = local_tgt * lax.axis_size("tgt")
    block_rows = math.gcd(local_src, 128)
    nblocks = local_src // block_rows
    sq_tgt = jnp.sum(tgt_rows * tgt_rows, axis=1)
    sq_src = jnp.sum(src_rows * src_rows, axis=1)
    inner = jnp.dot(
        src_rows, tgt_rows.T, precision=lax.Precision.HIGHEST, preferred_element_type=jnp.float32
    )
    cost_tile = sq_src[:, None] + sq_tgt[None, :] - 2.0 * inner
    cost_blocks = cost_tile.reshape(nblocks, block_rows, local_tgt)

    def row_pass(cost_blk):
        scores = (potential_in[None, :] - cost_blk) / epsilon
        top = jnp.max(scores, axis=1)
        return (top, jnp.sum(jnp.exp(scores - top[:, None]), axis=1))

    row_top, row_total = lax.map(row_pass, cost_blocks)
    row_top, row_total = joined(
        (row_top.reshape(local_src), row_total.reshape(local_src)), "tgt", lse_combine
    )
    source_potential = -epsilon * jnp.log(jnp.float32(num_src)) - epsilon * (
        row_top + jnp.log(row_total)
    )
    pot_blocks = source_potential.reshape(nblocks, block_rows)

    def column_step(running, inputs):
        cost_blk, pot_blk = inputs
        scores = (pot_blk[:, None] - cost_blk) / epsilon
        top = jnp.max(scores, axis=0)
        total = jnp.sum(jnp.exp(scores - top[None, :]), axis=0)
        return (lse_combine(running, (top, total)), None)

    start = (jnp.full((local_tgt,), -jnp.inf, jnp.float32), jnp.zeros((local_tgt,), jnp.float32))
    (col_top, col_total), _ = lax.scan(column_step, start, (cost_blocks, pot_blocks))
    log_tgt = jnp.log(jnp.float32(num_tgt))
    col_top, col_total = joined((col_top, col_total), "src", lse_combine)
    target_potential = -epsilon * log_tgt - epsilon * (col_top + jnp.log(col_total))

    def map_pass(cost_blk):
        scores = (target_potential[None, :] - cost_blk) / epsilon
        top = jnp.max(scores, axis=1)
        weights = jnp.exp(scores - top[:, None])
        total = jnp.sum(weights, axis=1)
        summed = jnp.dot(
            weights, tgt_rows, precision=lax.Precision.HIGHEST, preferred_element_type=jnp.float32
        )
        return (top, total, summed)

    map_top, map_total, map_summed = lax.map(map_pass, cost_blocks)
    map_top = map_top.reshape(local_src)
    map_total = map_total.reshape(local_src)
    map_summed = map_summed.reshape(local_src, width)
    share_rows = local_src // lax.axis_size("tgt")
    map_top, map_total, map_summed = joined((map_top, map_total, map_summed), "tgt", map_combine)
    whole_map = map_summed / map_total[:, None]
    mapped = lax.dynamic_slice_in_dim(whole_map, lax.axis_index("tgt") * share_rows, share_rows)
    return (source_potential, target_potential, mapped)


def solution(mesh):
    placed = (P(("src", "tgt"), None), P(("tgt", "src"), None), P("tgt"))
    return jax.shard_map(
        per_device,
        mesh=mesh,
        in_specs=placed,
        out_specs=(P("src"), P("tgt"), P(("src", "tgt"), None)),
        check_vma=False,
    )
```

profile of v0, /device:TPU:1, one launch (start us, length us, event | category | flops | bytes accessed | tf_op | source)
XLA Modules:
  0.0 541.5 jit_solution(12576757539892724005)
XLA Ops:
  8.0 24.1 %all_gather.33 = f32[1024,128]{1,0:T(8,128)S(1)} all-gather(f32[128,128]{1,0:T(8,128)} %param.15), channel_id=1, replica_groups=mesh['src'=32,'tgt'=8] {'tgt'}, dimensions={0}, use_global_device_ids=true | all-gather | bytes 589824 | tf_op jit(solution)/shard_map/all_gather | solution.py:38
  32.3 33.6 %all-gather.11.cloned.1.call-done = f32[8192,128]{1,0:T(8,128)} async-done(((f32[256,128]{1,0:T(8,128)}), f32[8192,128]{1,0:T(8,128)}) %all-gather.11.cloned.1.call-update) | async-done | bytes 4194320 | tf_op jit(solution)/shard_map/all_gather | solution.py:39
  65.9 3.5 multiply_reduce_fusion
  69.4 31.2 %multiply_subtract_fusion = f32[1024,8192]{1,0:T(8,128)} fusion(f32[8192]{0:T(1024)S(1)} %multiply_reduce_fusion, f32[1024]{0:T(1024)S(1)} %multiply_reduce_fusion.1, f32[1024,128]{1,0:T(8,128)S(1)} %all_gather.33, f32[8192,128]{1,0:T(8,128)S(1)} %copy-done), kind=kOutput, calls=%fused_computation.38 | convolution fusion | flops 12910067712 | bytes 38309888 | tf_op jit(solution)/shard_map/dot_general | solution.py:49
  100.6 47.2 %while.92 = (s32[]{:T(128)}, f32[8,128]{1,0:T(8,128)S(1)}, f32[8,128]{1,0:T(8,128)S(1)}, f32[8192]{0:T(1024)S(1)}, f32[8,128,8192]{2,1,0:T(8,128)}, /*index=5*/s32[]{:T(128)}, s32[]{:T(128)}) while((s32[]{:T(128)}, f32[8,128]{1,0:T(8,128)S(1)}, f32[8,128]{1,0:T(8,128)S(1)}, f32[8192]{0:T(1024)S(1)}, f32[8,128,8192]{2,1,0:T(8,128)}, ...), condition=%wide.region_5.6_spmd, body=%wide.region_2.5_spmd.sunk | while | flops 7339778 | bytes 8457829 | solution.py:60
  147.8 19.5 %all-gather.2 = f32[8,1,1024]{2,1,0:T(1,128)S(1)} all-gather(f32[1,1,1024]{2,1,0:T(1,128)S(1)} %bitcast.143), channel_id=1, replica_groups=mesh['src'=32,'tgt'=8] {'tgt'}, dimensions={0}, use_global_device_ids=true | all-gather | bytes 36864 | tf_op jit(solution)/shard_map/all_gather | solution.py:12
  167.4 18.3 %all-gather.3 = f32[8,1,1024]{2,1,0:T(1,128)S(1)} all-gather(f32[1,1,1024]{2,1,0:T(1,128)S(1)} %bitcast.144), channel_id=1, replica_groups=mesh['src'=32,'tgt'=8] {'tgt'}, dimensions={0}, use_global_device_ids=true | all-gather | bytes 36864 | tf_op jit(solution)/shard_map/all_gather | solution.py:12
  186.1 47.5 %while.97 = (s32[]{:T(128)}, f32[8192]{0:T(1024)S(1)}, f32[8192]{0:T(1024)S(1)}, f32[8,128]{1,0:T(8,128)S(1)}, f32[8,128,8192]{2,1,0:T(8,128)}, /*index=5*/s32[]{:T(128)}, s32[]{:T(128)}) while((s32[]{:T(128)}, f32[8192]{0:T(1024)S(1)}, f32[8192]{0:T(1024)S(1)}, f32[8,128]{1,0:T(8,128)S(1)}, f32[8,128,8192]{2,1,0:T(8,128)}, ...), condition=%wide.region_11.12_spmd.clone, body=%wide.region_8.11_spmd.clone.sunk | while | flops 7389187 | bytes 8685675 | solution.py:77
  235.0 57.9 %all-gather.15.cloned.1.call-done = f32[262144]{0:T(1024)} async-done(((f32[8192]{0:T(1024)}), f32[262144]{0:T(1024)}) %all-gather.15.cloned.1.call-update) | async-done | bytes 1048592 | tf_op jit(solution)/shard_map/all_gather | solution.py:12
  294.4 48.9 %all-gather.17.cloned.1.call-done = f32[262144]{0:T(1024)} async-done(((f32[8192]{0:T(1024)}), f32[262144]{0:T(1024)}) %all-gather.17.cloned.1.call-update) | async-done | bytes 1048592 | tf_op jit(solution)/shard_map/all_gather | solution.py:12
  345.4 3.8 while.94
  349.2 118.5 %while.95 = (s32[]{:T(128)}, f32[8,128]{1,0:T(8,128)S(1)}, f32[8,128]{1,0:T(8,128)S(1)}, f32[8,128,128]{2,1,0:T(8,128)}, f32[8192]{0:T(1024)S(1)}, /*index=5*/f3...) while((s32[]{:T(128)}, f32[8,128]{1,0:T(8,128)S(1)}, f32[8,128]{1,0:T(8,128)S(1)}, ...), condition=%wide.region_17.18_spmd, body=%wide.region_14.17_spmd.sunk | while | flops 1621098240 | bytes 16946292 | solution.py:92
  355.1 8.9 %fusion.33 = f32[8,128,128]{2,1,0:T(8,128)} fusion(f32[8,128,128]{2,1,0:T(8,128)} %get-tuple-element.1000, s32[]{:T(128)S(6)} %copy.63, f32[8192,128]{1,0:T(8,128)} %get-tuple-element.1012, f32[8,128,8192]{2,1,0:T(8,128)} %get-tuple-element.1011, f32[128]{0:T(128)S(1)} %fusion.31, f32[8192]{0:T(1024)S(1)} %get-tuple-element.1010), kind=kOutput, calls=%fused_computation.20.clone.1 | convolution fusion | flops 1613758464 | bytes 8488448 | tf_op jit(solution)/shard_map/while/body/eval_jaxpr/dot_general | solution.py:87
  370.0 8.9 %fusion.33 = f32[8,128,128]{2,1,0:T(8,128)} fusion(f32[8,128,128]{2,1,0:T(8,128)} %get-tuple-element.1000, s32[]{:T(128)S(6)} %copy.63, f32[8192,128]{1,0:T(8,128)} %get-tuple-element.1012, f32[8,128,8192]{2,1,0:T(8,128)} %get-tuple-element.1011, f32[128]{0:T(128)S(1)} %fusion.31, f32[8192]{0:T(1024)S(1)} %get-tuple-element.1010), kind=kOutput, calls=%fused_computation.20.clone.1 | convolution fusion | flops 1613758464 | bytes 8488448 | tf_op jit(solution)/shard_map/while/body/eval_jaxpr/dot_general | solution.py:87
  384.8 8.9 %fusion.33 = f32[8,128,128]{2,1,0:T(8,128)} fusion(f32[8,128,128]{2,1,0:T(8,128)} %get-tuple-element.1000, s32[]{:T(128)S(6)} %copy.63, f32[8192,128]{1,0:T(8,128)} %get-tuple-element.1012, f32[8,128,8192]{2,1,0:T(8,128)} %get-tuple-element.1011, f32[128]{0:T(128)S(1)} %fusion.31, f32[8192]{0:T(1024)S(1)} %get-tuple-element.1010), kind=kOutput, calls=%fused_computation.20.clone.1 | convolution fusion | flops 1613758464 | bytes 8488448 | tf_op jit(solution)/shard_map/while/body/eval_jaxpr/dot_general | solution.py:87
  399.6 8.9 %fusion.33 = f32[8,128,128]{2,1,0:T(8,128)} fusion(f32[8,128,128]{2,1,0:T(8,128)} %get-tuple-element.1000, s32[]{:T(128)S(6)} %copy.63, f32[8192,128]{1,0:T(8,128)} %get-tuple-element.1012, f32[8,128,8192]{2,1,0:T(8,128)} %get-tuple-element.1011, f32[128]{0:T(128)S(1)} %fusion.31, f32[8192]{0:T(1024)S(1)} %get-tuple-element.1010), kind=kOutput, calls=%fused_computation.20.clone.1 | convolution fusion | flops 1613758464 | bytes 8488448 | tf_op jit(solution)/shard_map/while/body/eval_jaxpr/dot_general | solution.py:87
  414.4 8.9 %fusion.33 = f32[8,128,128]{2,1,0:T(8,128)} fusion(f32[8,128,128]{2,1,0:T(8,128)} %get-tuple-element.1000, s32[]{:T(128)S(6)} %copy.63, f32[8192,128]{1,0:T(8,128)} %get-tuple-element.1012, f32[8,128,8192]{2,1,0:T(8,128)} %get-tuple-element.1011, f32[128]{0:T(128)S(1)} %fusion.31, f32[8192]{0:T(1024)S(1)} %get-tuple-element.1010), kind=kOutput, calls=%fused_computation.20.clone.1 | convolution fusion | flops 1613758464 | bytes 8488448 | tf_op jit(solution)/shard_map/while/body/eval_jaxpr/dot_general | solution.py:87
  429.2 8.9 %fusion.33 = f32[8,128,128]{2,1,0:T(8,128)} fusion(f32[8,128,128]{2,1,0:T(8,128)} %get-tuple-element.1000, s32[]{:T(128)S(6)} %copy.63, f32[8192,128]{1,0:T(8,128)} %get-tuple-element.1012, f32[8,128,8192]{2,1,0:T(8,128)} %get-tuple-element.1011, f32[128]{0:T(128)S(1)} %fusion.31, f32[8192]{0:T(1024)S(1)} %get-tuple-element.1010), kind=kOutput, calls=%fused_computation.20.clone.1 | convolution fusion | flops 1613758464 | bytes 8488448 | tf_op jit(solution)/shard_map/while/body/eval_jaxpr/dot_general | solution.py:87
  444.0 8.9 %fusion.33 = f32[8,128,128]{2,1,0:T(8,128)} fusion(f32[8,128,128]{2,1,0:T(8,128)} %get-tuple-element.1000, s32[]{:T(128)S(6)} %copy.63, f32[8192,128]{1,0:T(8,128)} %get-tuple-element.1012, f32[8,128,8192]{2,1,0:T(8,128)} %get-tuple-element.1011, f32[128]{0:T(128)S(1)} %fusion.31, f32[8192]{0:T(1024)S(1)} %get-tuple-element.1010), kind=kOutput, calls=%fused_computation.20.clone.1 | convolution fusion | flops 1613758464 | bytes 8488448 | tf_op jit(solution)/shard_map/while/body/eval_jaxpr/dot_general | solution.py:87
  458.8 8.9 %fusion.33 = f32[8,128,128]{2,1,0:T(8,128)} fusion(f32[8,128,128]{2,1,0:T(8,128)} %get-tuple-element.1000, s32[]{:T(128)S(6)} %copy.63, f32[8192,128]{1,0:T(8,128)} %get-tuple-element.1012, f32[8,128,8192]{2,1,0:T(8,128)} %get-tuple-element.1011, f32[128]{0:T(128)S(1)} %fusion.31, f32[8192]{0:T(1024)S(1)} %get-tuple-element.1010), kind=kOutput, calls=%fused_computation.20.clone.1 | convolution fusion | flops 1613758464 | bytes 8488448 | tf_op jit(solution)/shard_map/while/body/eval_jaxpr/dot_general | solution.py:87
  467.8 20.7 %all-gather.4 = f32[8,1,1024]{2,1,0:T(1,128)S(1)} all-gather(f32[1,1,1024]{2,1,0:T(1,128)S(1)} %bitcast.141), channel_id=1, replica_groups=mesh['src'=32,'tgt'=8] {'tgt'}, dimensions={0}, use_global_device_ids=true | all-gather | bytes 36864 | tf_op jit(solution)/shard_map/all_gather | solution.py:12
  488.6 20.5 %all-gather.5 = f32[8,1,1024]{2,1,0:T(1,128)S(1)} all-gather(f32[1,1,1024]{2,1,0:T(1,128)S(1)} %bitcast.142), channel_id=1, replica_groups=mesh['src'=32,'tgt'=8] {'tgt'}, dimensions={0}, use_global_device_ids=true | all-gather | bytes 36864 | tf_op jit(solution)/shard_map/all_gather | solution.py:12
  509.1 13.1 %all-gather.13.cloned.1.call-done = f32[8,1024,128]{2,1,0:T(8,128)} async-done(((f32[1,1024,128]{2,1,0:T(8,128)}), f32[8,1024,128]{2,1,0:T(8,128)}) %all-gather.13.cloned.1.call-update) | async-done | bytes 4194320 | tf_op jit(solution)/shard_map/all_gather | solution.py:12
  523.3 10.9 %while.96 = (s32[]{:T(128)}, f32[1024]{0:T(1024)S(1)}, f32[1024]{0:T(1024)S(1)}, f32[1024,128]{1,0:T(8,128)S(1)}, f32[8,1024]{1,0:T(8,128)S(1)}, /*index=5*/f32[...) while((s32[]{:T(128)}, f32[1024]{0:T(1024)S(1)}, f32[1024]{0:T(1024)S(1)}, ...), condition=%wide.region_19.20_spmd, body=%wide.region_18.19_spmd.sunk | while | flops 399365 | bytes 1630359 | solution.py:18
  (240 shorter events, 163.3 us)
Async XLA Ops:
  7.2 58.7 %all-gather.11.cloned.1.call-start = ((), (), s32[]{:S(2)}) async-start(), calls=%async_computation | async-start | bytes 4325376 | tf_op jit(solution)/shard_map/all_gather | solution.py:39
  7.9 285.0 %all-gather.15.cloned.1.call-start = ((), (), s32[]{:S(2)}) async-start(), calls=%async_computation.2 | async-start | bytes 1081344 | tf_op jit(solution)/shard_map/all_gather | solution.py:12
  65.9 3.5 copy-start
  69.4 31.2 %copy-start.2 = (f32[8192]{0:T(1024)S(1)}, f32[8192]{0:T(1024)}, u32[]{:S(2)}) copy-start(f32[8192]{0:T(1024)} %param.17) | copy-start | bytes 98308
  233.6 0.6 copy-start.3
  233.6 0.7 copy-start.4
  233.6 115.6 %copy-start.5 = (f32[8,128]{1,0:T(8,128)}, f32[8,128]{1,0:T(8,128)S(1)}, u32[]{:S(2)}) copy-start(f32[8,128]{1,0:T(8,128)S(1)} %get-tuple-element.1064) | copy-start | bytes 12292
  234.2 109.0 %all-gather.17.cloned.1.call-start = ((), (), s32[]{:S(2)}) async-start(), calls=%async_computation.3 | async-start | bytes 1081344 | tf_op jit(solution)/shard_map/all_gather | solution.py:12
  234.9 287.2 %all-gather.13.cloned.1.call-start = ((), (), s32[]{:S(2)}) async-start(), calls=%async_computation.1 | async-start | bytes 4718592 | tf_op jit(solution)/shard_map/all_gather | solution.py:12
  292.9 52.5 %slice-start = ((f32[262144]{0:T(1024)}), f32[8192]{0:T(1024)S(1)}, s32[]{:S(2)}) async-start(f32[262144]{0:T(1024)} %all-gather.15.cloned.1.call-done), calls=%async_computation.4 | async-start | bytes 65536 | tf_op jit(solution)/shard_map/slice | solution.py:13
  467.8 55.5 %copy-start.1 = (f32[8192]{0:T(1024)}, f32[8192]{0:T(1024)S(1)}, u32[]{:S(2)}) copy-start(f32[8192]{0:T(1024)S(1)} %get-tuple-element.1052) | copy-start | bytes 98308
Sparse Core Ops, SparseCore 0:
  10.6 55.2 all-gather.10
  234.3 58.5 all-gather.14
  296.0 47.1 all-gather.16
  467.9 54.2 all-gather.12
where the time goes:
time: 544 us; the launch traced here: 542 us
  other arithmetic  156 us (29%)
  waiting for transfers between devices  155 us (28%)
  blocking collectives  103 us (19%)
  matrix products  103 us (19%)
  between operations  14 us (3%)
  local copies, waits for them, and re-layouts  8.36 us (2%)
    all_gather x3, waiting for transfers between devices, joined(): everything = jax.tree.map(lambda part: lax.all_gather(part, axis), array)  120 us
    all_gather x4, blocking collectives, joined(): everything = jax.tree.map(lambda part: lax.all_gather(part, axis), array)  79.1 us
    dot_general x8, matrix products, map_pass(): jnp.dot(weights, tgt_rows, precision=lax.Precision.HIGHEST, preferred_ele...  71.4 us
    all_gather x1, waiting for transfers between devices, per_device(): tgt_rows = lax.all_gather(targets, 'src', axis=0, tiled=True)  33.6 us
    dot_general x1, matrix products, per_device(): jnp.dot(src_rows, tgt_rows.T, precision=lax.Precision.HIGHEST, preferred_...  31.2 us
    reduce_sum x8, other arithmetic, row_pass(): return (top, jnp.sum(jnp.exp(scores - top[:, None]), axis=1))  25.1 us
    reduce_sum x8, other arithmetic, map_pass(): total = jnp.sum(weights, axis=1)  25.1 us
    reduce_sum x8, other arithmetic, column_step(): total = jnp.sum(jnp.exp(scores - top[None, :]), axis=0)  25 us
  transfers between devices with their start and end apart: 4, of which 4 were waited for; matrix products, arithmetic and copies ran while one was open for 0% of the time, Pallas kernels for 0%

commit v1 on v0

v1 whole, which is shorter than its diff:
```python
import math

import jax
import jax.numpy as jnp
from jax import lax
from jax.experimental import pallas as pl
from jax.experimental.pallas import tpu as pltpu
from jax.sharding import PartitionSpec as P

epsilon = 0.05
LN2 = math.log(2.0)
ALPHA = 1.0 / (epsilon * LN2)
MESH = pl.DeviceIdType.MESH
F32 = jnp.float32
BF16 = jnp.bfloat16
NSRC = 32
NTGT = 8
SIDE = 4
PAIR = 2 * SIDE
LAG = 3
ORDER = (1, 7, 2, 6, 0, 4, 3, 5)
EARLY = 640


def gray(i):
    return i + i // 2 - 2 * (i // 3)


def kernel(
    src_ref, tgt_ref, pot_ref, sp_ref, tp_ref, map_ref,
    sbuf, tbuf, lhs, cols, scores, top, total, rslot, rrow, rcol,
    lsend, lrecv, call, colmax, acc, den, psend, msend, precv, mrecv,
    z_send, z_recv, p1_send, p2_send, half_send, sib_send, t_recv, sib_recv,
    r_send, r_recv, l_send, l_recv, c_send, c_recv, m_send, m_recv,
):
    me = lax.axis_index("src")
    z = lax.axis_index("tgt")
    core = me % 2
    chip = me // 2
    x = chip % SIDE
    y = chip // SIDE
    sib = me + 1 - 2 * core

    def on_src(i):
        return {"src": i}

    def on_tgt(i):
        return {"tgt": (i + NTGT) % NTGT}

    def rcopy(src, dst, send, recv, dev):
        return pltpu.make_async_remote_copy(
            src_ref=src, dst_ref=dst, send_sem=send, recv_sem=recv, device_id=dev, device_id_type=MESH
        )

    bar = pltpu.get_barrier_semaphore()

    def greet_src(i, carry):
        pl.semaphore_signal(bar, inc=1, device_id=on_src((me + i) % NSRC), device_id_type=MESH)
        return carry

    def greet_tgt(i, carry):
        pl.semaphore_signal(bar, inc=1, device_id=on_tgt(z + i), device_id_type=MESH)
        return carry

    lax.fori_loop(1, NSRC, greet_src, 0)
    lax.fori_loop(1, NTGT, greet_tgt, 0)

    for h in range(2):
        tbuf[chip, core, h] = tgt_ref[pl.ds(h * 128, 128), :]
    sbuf[0] = src_ref[...]

    lane = lax.broadcasted_iota(jnp.int32, (128, 128), 1)
    row = lax.broadcasted_iota(jnp.int32, (128, 128), 0)
    eye = lane == row

    def split3(a):
        a1 = a.astype(BF16).astype(F32)
        rest = a - a1
        a2 = rest.astype(BF16).astype(F32)
        return a1, a2, rest - a2

    def prep_src(place, d):
        s = sbuf[d]
        scaled = s * (2.0 * ALPHA)
        hi = scaled.astype(BF16)
        lo = (scaled - hi.astype(F32)).astype(BF16)
        b1, b2, b3 = split3(-ALPHA * jnp.sum(s * s, axis=1, keepdims=True))
        extra = jnp.where(lane == 0, b1, jnp.where(lane == 1, b2, jnp.where(lane == 2, b3, jnp.where(lane < 6, 1.0, 0.0))))
        rows = pl.ds(place * 128, 128)
        lhs[rows, 0:128] = hi
        lhs[rows, 128:256] = hi
        lhs[rows, 256:384] = lo
        lhs[rows, 384:512] = extra.astype(BF16)

    def prep_tgt(u, q, h):
        for c in range(2):
            t = tbuf[q, c, h]
            pot = pot_ref[pl.ds(q * 4 + c * 2 + h, 1), :]
            hi = t.astype(BF16)
            lo = (t - hi.astype(F32)).astype(BF16)
            a1, a2, a3 = split3(ALPHA * jnp.sum(jnp.where(eye, pot, 0.0) - t * t, axis=1, keepdims=True))
            extra = jnp.where(lane < 3, 1.0, jnp.where(lane == 3, a1, jnp.where(lane == 4, a2, jnp.where(lane == 5, a3, 0.0))))
            rows = pl.ds(c * 128, 128)
            cols[u, rows, 0:128] = lo
            cols[u, rows, 128:256] = hi
            cols[u, rows, 256:384] = hi
            cols[u, rows, 384:512] = extra.astype(BF16)

    prep_src(ORDER.index(0), 0)
    top[...] = jnp.full((1024, 128), -jnp.inf, F32)
    total[...] = jnp.zeros((1024, 128), F32)
    pl.semaphore_wait(bar, NSRC + NTGT - 2)

    def at(xx, yy):
        return (((yy + SIDE) % SIDE) * SIDE + (xx + SIDE) % SIDE) * 2 + core

    def p1_copy(h, i):
        step = 1 - 2 * i
        dev = on_src(at(x + step * (1 - h), y + step * h))
        piece = tbuf.at[chip, core, h]
        return rcopy(piece, piece, p1_send.at[h * 2 + i], t_recv.at[0, h * 16 + chip], dev)

    def z_copy(hop, i):
        d = (NTGT - hop) % NTGT if i == 0 else hop
        to = (d + NTGT - 1) % NTGT if i == 0 else (d + 1) % NTGT
        dev = on_tgt(z + 1 if i == 0 else z - 1)
        if hop < 3:
            return rcopy(sbuf.at[d], sbuf.at[to], z_send.at[hop * 2 + i], z_recv.at[to], dev)
        rows = pl.ds(i * 64, 64)
        return rcopy(sbuf.at[d, rows], sbuf.at[to, rows], z_send.at[hop * 2 + i], z_recv.at[to + 4 * i], dev)

    for h in range(2):
        for i in range(2):
            p1_copy(h, i).start()
    for i in range(2):
        z_copy(0, i).start()

    def z_arrive(hop):
        if hop < 4:
            for i, d in enumerate((NTGT - hop, hop)):
                rcopy(sbuf.at[d], sbuf.at[d], z_send.at[0], z_recv.at[d], on_tgt(z + 1)).wait_recv()
                z_copy(hop, i).start()
            for d in (NTGT - hop, hop):
                prep_src(ORDER.index(d), d)
        else:
            for i in range(2):
                part = sbuf.at[4, pl.ds(i * 64, 64)]
                rcopy(part, part, z_send.at[0], z_recv.at[4 + 4 * i], on_tgt(z + 1)).wait_recv()
            prep_src(ORDER.index(4), 4)

    def place_of(m, h):
        late = (m + 12) // 16
        d1 = gray((1 - late) * m + late * ((m + 8) // 3 - 4))
        d2 = gray(late * ((m + 8) % 3 + 1))
        dx = (1 - h) * d1 + h * d2
        dy = (1 - h) * d2 + h * d1
        q = ((y + dy) % SIDE) * SIDE + (x + dx) % SIDE
        return d1, d2, q

    def p2_copy(m, h, q, i):
        step = 1 - 2 * i
        dev = on_src(at(x + step * h, y + step * (1 - h)))
        piece = tbuf.at[q, core, h]
        return rcopy(piece, piece, p2_send.at[m * 4 + h * 2 + i], t_recv.at[0, h * 16 + q], dev)

    def half_copy(m, h, q, d1, d2):
        d = d1 + d2 if isinstance(d1, int) else d1 * (1 - (d2 + 3) // 4) + d2
        second = (d2 + 3) // 4
        step = d - 2
        axis = (second + h) % 2
        part = (3 - d) // 2
        dev = on_src(at(x + step * (1 - axis), y + step * axis))
        piece = tbuf.at[q, core, h, pl.ds(pl.multiple_of(part * 64, 64), 64)]
        return rcopy(piece, piece, half_send.at[m * 2 + h], t_recv.at[part, h * 16 + q], dev)

    def sib_copy(m, h, q):
        piece = tbuf.at[q, core, h]
        return rcopy(piece, piece, sib_send.at[m * 2 + h], sib_recv.at[h * 16 + q], on_src(sib))

    def is_half(d1, d2):
        return (d2 % 2) + (1 - (d2 + 3) // 4) * (d1 % 2)

    def in_parts(d1, d2):
        return (d2 // 2) * (1 - d2 % 2) + (1 - (d2 + 3) // 4) * (d1 // 2) * (1 - d1 % 2)

    def gather_step(m):
        for h in range(2):
            d1, d2, q = place_of(m, h)
            parts = in_parts(d1, d2)
            piece = tbuf.at[q, core, h]

            @pl.when(jnp.logical_and(m > 0, parts == 0))
            def _():
                rcopy(piece, piece, sib_send.at[0], t_recv.at[0, h * 16 + q], on_src(sib)).wait_recv()

            @pl.when(parts == 1)
            def _():
                for i in range(2):
                    part = tbuf.at[q, core, h, pl.ds(i * 64, 64)]
                    rcopy(part, part, sib_send.at[0], t_recv.at[i, h * 16 + q], on_src(sib)).wait_recv()

            @pl.when(is_half(d1, d2) == 1)
            def _():
                half_copy(m, h, q, d1, d2).start()

            @pl.when(m < 4)
            def _():
                for i in range(2):
                    p2_copy(m, h, q, i).start()

            sib_copy(m, h, q).start()

    def score_rows(m, r0, n):
        us = []
        for h in range(2):
            _, _, q = place_of(m, h)
            u = q * 2 + h
            us.append(u)
            scores[u, pl.ds(r0, n), :] = lax.dot_general(
                lhs[pl.ds(r0, n), :], cols[u], (((1,), (1,)), ((), ())), preferred_element_type=F32
            )
        for r in range(r0, r0 + n, 64):
            rows = pl.ds(r, 64)
            parts = [scores[u, rows, pl.ds(k * 128, 128)] for u in us for k in range(2)]
            old = top[rows, :]
            new = jnp.maximum(jnp.maximum(parts[0], parts[1]), jnp.maximum(parts[2], parts[3]))
            new = jnp.maximum(old, new)
            e = [jnp.exp2(p - new) for p in parts]
            total[rows, :] = total[rows, :] * jnp.exp2(old - new) + ((e[0] + e[1]) + (e[2] + e[3]))
            top[rows, :] = new

    def first_pass(m, carry):
        @pl.when(m < 16)
        def _():
            gather_step(m)

        for hop in range(1, 5):

            @pl.when(m == hop - 1)
            def _():
                z_arrive(hop)

        p = m - 2

        @pl.when(p >= 0)
        def _():
            for h in range(2):
                _, _, q = place_of(p, h)
                piece = tbuf.at[q, 1 - core, h]
                rcopy(piece, piece, sib_send.at[0], sib_recv.at[h * 16 + q], on_src(sib)).wait_recv()
                prep_tgt(q * 2 + h, q, h)
            score_rows(p, 0, EARLY)

        @pl.when(p >= PAIR)
        def _():
            def both(i, c):
                score_rows(p - PAIR + PAIR * i, EARLY, 1024 - EARLY)
                return c

            lax.fori_loop(0, 2, both, 0)

        return carry

    lax.fori_loop(0, 18, first_pass, 0)

    for place, d in enumerate(ORDER):
        rows = pl.ds(place * 128, 128)
        m = top[rows, :]
        high = jnp.max(m, axis=1, keepdims=True)
        s = jnp.sum(total[rows, :] * jnp.exp2(m - high), axis=1, keepdims=True)
        r = high + jnp.log2(s)
        rslot[z, pl.ds((z + d) % NTGT, 1), :] = jnp.sum(jnp.where(eye, r, 0.0), axis=0, keepdims=True)

    def r_copy(i):
        return rcopy(rslot.at[z], rslot.at[z], r_send.at[i], r_recv.at[z], on_tgt(z + i))

    for i in range(1, NTGT):
        r_copy(i).start()

    for h in range(2):
        for i in range(2):
            p1_copy(h, i).wait_send()
    for hop in range(4):
        for i in range(2):
            z_copy(hop, i).wait_send()

    def gather_sent(m, carry):
        for h in range(2):
            d1, d2, q = place_of(m, h)

            @pl.when(is_half(d1, d2) == 1)
            def _():
                half_copy(m, h, q, d1, d2).wait_send()

            @pl.when(m < 4)
            def _():
                for i in range(2):
                    p2_copy(m, h, q, i).wait_send()

            sib_copy(m, h, q).wait_send()
        return carry

    lax.fori_loop(0, 16, gather_sent, 0)

    for i in range(1, NTGT):
        other = (z + i) % NTGT
        slot = rslot.at[other]
        rcopy(slot, slot, r_send.at[0], r_recv.at[other], on_tgt(z + i)).wait_recv()
    slots = [rslot[i] for i in range(NTGT)]
    high = slots[0]
    for s in slots[1:]:
        high = jnp.maximum(high, s)
    sums = jnp.exp2(slots[0] - high)
    for s in slots[1:]:
        sums = sums + jnp.exp2(s - high)
    r_all = high + jnp.log2(sums)
    rrow[...] = r_all
    sp_ref[...] = -epsilon * math.log(NSRC * 1024) - (epsilon * LN2) * r_all
    for place, d in enumerate(ORDER):
        one = rrow[pl.ds((z + d) % NTGT, 1), :]
        rcol[pl.ds(place * 128, 128), :] = jnp.transpose(jnp.broadcast_to(one, (128, 128)))

    def l_copy(u):
        return rcopy(lsend.at[u], lrecv.at[me], l_send.at[u], l_recv.at[me], on_src(u))

    def c_copy(i):
        return rcopy(call.at[me], call.at[me], c_send.at[i], c_recv.at[me], on_src((me + i) % NSRC))

    def column_unit(u):
        step = 32
        high = None
        for r in range(0, 1024, step):
            rows = pl.ds(r, step)
            rc = rcol[rows, :]
            v = [scores[u, rows, pl.ds(k * 128, 128)] - rc for k in range(2)]
            high = v if high is None else [jnp.maximum(a, b) for a, b in zip(high, v)]
        high = [jnp.max(a, axis=0, keepdims=True) for a in high]
        sums = None
        for r in range(0, 1024, step):
            rows = pl.ds(r, step)
            rc = rcol[rows, :]
            e = [jnp.exp2((scores[u, rows, pl.ds(k * 128, 128)] - rc) - high[k]) for k in range(2)]
            for k in range(2):
                scores[u, rows, pl.ds(k * 128, 128)] = e[k]
            sums = e if sums is None else [a + b for a, b in zip(sums, e)]
        for k in range(2):
            part = pl.ds(k * 128, 128)
            colmax[u, :, part] = high[k]
            lsend[u, :, part] = high[k] + jnp.log2(jnp.sum(sums[k], axis=0, keepdims=True))

        @pl.when(u != me)
        def _():
            l_copy(u).start()

        @pl.when(u == me)
        def _():
            lrecv[me] = lsend[u]

    def column_total():
        def arrived(i, carry):
            other = (me + i) % NSRC
            slot = lrecv.at[other]
            rcopy(slot, slot, l_send.at[0], l_recv.at[other], on_src(other)).wait_recv()
            return carry

        lax.fori_loop(1, NSRC, arrived, 0)
        parts = lrecv[...]
        high = jnp.max(parts, axis=0)
        call[me] = high + jnp.log2(jnp.sum(jnp.exp2(parts - high[None]), axis=0))

        def tell(i, carry):
            c_copy(i).start()
            return carry

        lax.fori_loop(1, NSRC, tell, 0)

    def second_pass(k, carry):
        @pl.when(k < NSRC)
        def _():
            column_unit(k)

        @pl.when(k == me + LAG)
        def _():
            column_total()

        return carry

    lax.fori_loop(0, NSRC + LAG, second_pass, 0)

    def map_group(r0, first):
        rows = pl.ds(r0, 256)
        acc[...] = jnp.zeros((256, 256), F32)
        den[...] = jnp.zeros((256, 128), F32)

        def unit(u, carry):
            if first:

                @pl.when(u != me)
                def _():
                    slot = call.at[u]
                    rcopy(slot, slot, c_send.at[0], c_recv.at[u], on_src(u)).wait_recv()

            f = jnp.exp2(colmax[u] - call[u])
            w = scores[u, rows, :] * f
            den[...] += w[:, :128] + w[:, 128:]
            hi = w.astype(BF16)
            lo = (w - hi.astype(F32)).astype(BF16)
            t = cols[u, :, 0:256]
            acc[...] += jnp.dot(hi, t, preferred_element_type=F32) + jnp.dot(lo, t, preferred_element_type=F32)
            return carry

        lax.fori_loop(0, NSRC, unit, 0)
        out = []
        for i in range(2):
            part = pl.ds(i * 128, 128)
            d = jnp.sum(den[part, :], axis=1, keepdims=True)
            out.append((acc[part, 0:128] + acc[part, 128:256], jnp.sum(jnp.where(eye, d, 0.0), axis=0, keepdims=True)))
        return out

    def put(buf, pair, extra=None, lo=0, hi=136):
        num, d = pair
        d = jnp.broadcast_to(d, (8, 128))
        if extra is None:
            buf[0:128, :] = num
            buf[128:136, :] = d
            return
        if lo == 0:
            n = min(hi, 128)
            buf[0:n, :] = num[0:n] + extra[0:n, :]
            if n < 128:
                buf[n:128, :] = num[n:128]
        else:
            buf[0:lo, :] = num[0:lo]
            buf[lo:128, :] = num[lo:128] + extra[lo:128, :]
        buf[128:136, :] = d + extra[128:136, :] if hi == 136 else d

    halves = (pl.ds(0, 64), pl.ds(64, 72))

    def plus(hop):
        rows = halves[0] if hop == 0 else pl.ds(0, 136)
        return rcopy(psend.at[hop, rows], precv.at[hop, rows], m_send.at[hop], m_recv.at[hop], on_tgt(z + 1))

    def minus(hop):
        rows = halves[1] if hop == 0 else pl.ds(0, 136)
        return rcopy(msend.at[hop, rows], mrecv.at[hop, rows], m_send.at[4 + hop], m_recv.at[4 + hop], on_tgt(z - 1))

    own, far = map_group(512, True)
    put(psend.at[0], far)
    put(msend.at[0], far)
    plus(0).start()
    minus(0).start()
    for hop, r0 in ((1, 768), (2, 256), (3, 0)):
        if hop == 1:
            own_num, own_den = own
            acc_own = own_num
        up, down = map_group(r0, False)
        plus(hop - 1).wait_recv()
        if hop == 1:
            put(psend.at[hop], up, precv.at[hop - 1], 0, 64)
        else:
            put(psend.at[hop], up, precv.at[hop - 1])
        plus(hop).start()
        minus(hop - 1).wait_recv()
        if hop == 1:
            put(msend.at[hop], down, mrecv.at[hop - 1], 64, 136)
        else:
            put(msend.at[hop], down, mrecv.at[hop - 1])
        minus(hop).start()

    for u in range(NSRC):
        for c in range(2):
            r = (u // 2) * 4 + c * 2 + u % 2
            tp_ref[r : r + 1, :] = (
                pot_ref[r : r + 1, :] - (epsilon * LN2) * call[u, :, c * 128 : (c + 1) * 128]
                - epsilon * math.log(NTGT * 8192 / (NSRC * 1024))
            )
    for i in range(1, NTGT):
        r_copy(i).wait_send()

    def small_sent(i, carry):
        c_copy(i).wait_send()
        l_copy((me + i) % NSRC).wait_send()
        return carry

    lax.fori_loop(1, NSRC, small_sent, 0)
    for hop in range(4):
        plus(hop).wait_send()
        minus(hop).wait_send()
    plus(3).wait_recv()
    minus(3).wait_recv()
    num = acc_own + precv[3, 0:128, :] + mrecv[3, 0:128, :]
    d = own_den + precv[3, 128:129, :] + mrecv[3, 128:129, :]
    d = jnp.sum(jnp.where(eye, d, 0.0), axis=1, keepdims=True)
    map_ref[...] = num / d


def per_device(sources, targets, potential_in):
    vmem = pl.BlockSpec(memory_space=pltpu.VMEM)
    dma = pltpu.SemaphoreType.DMA
    sp, tp, mapped = pl.pallas_call(
        kernel,
        out_shape=(
            jax.ShapeDtypeStruct((8, 128), F32),
            jax.ShapeDtypeStruct((64, 128), F32),
            jax.ShapeDtypeStruct((128, 128), F32),
        ),
        in_specs=[vmem] * 3,
        out_specs=(vmem,) * 3,
        scratch_shapes=[
            pltpu.VMEM((8, 128, 128), F32),
            pltpu.VMEM((16, 2, 2, 128, 128), F32),
            pltpu.VMEM((1024, 512), BF16),
            pltpu.VMEM((32, 256, 512), BF16),
            pltpu.VMEM((32, 1024, 256), F32),
            pltpu.VMEM((1024, 128), F32),
            pltpu.VMEM((1024, 128), F32),
            pltpu.VMEM((8, 8, 128), F32),
            pltpu.VMEM((8, 128), F32),
            pltpu.VMEM((1024, 128), F32),
            pltpu.VMEM((32, 1, 256), F32),
            pltpu.VMEM((32, 1, 256), F32),
            pltpu.VMEM((32, 1, 256), F32),
            pltpu.VMEM((32, 1, 256), F32),
            pltpu.VMEM((256, 256), F32),
            pltpu.VMEM((256, 128), F32),
            pltpu.VMEM((4, 136, 128), F32),
            pltpu.VMEM((4, 136, 128), F32),
            pltpu.VMEM((4, 136, 128), F32),
            pltpu.VMEM((4, 136, 128), F32),
            dma((8,)),
            dma((9,)),
            dma((4,)),
            dma((16,)),
            dma((32,)),
            dma((32,)),
            dma((2, 32)),
            dma((32,)),
            dma((8,)),
            dma((8,)),
            dma((32,)),
            dma((32,)),
            dma((32,)),
            dma((32,)),
            dma((8,)),
            dma((8,)),
        ],
        compiler_params=pltpu.CompilerParams(
            collective_id=0, has_side_effects=True, vmem_limit_bytes=62 * 1024 * 1024
        ),
        cost_estimate=pl.CostEstimate(
            flops=2 * 1024 * 8192 * 1024, bytes_accessed=1 << 20, transcendentals=2 * 1024 * 8192
        ),
    )(sources, targets, potential_in.reshape(64, 128))
    return sp.reshape(1024), tp.reshape(8192), mapped


def solution(mesh):
    return jax.shard_map(
        per_device,
        mesh=mesh,
        in_specs=(P(("src", "tgt"), None), P(("tgt", "src"), None), P("tgt")),
        out_specs=(P("src"), P("tgt"), P(("src", "tgt"), None)),
        check_vma=False,
    )
```

time: 544 us -> 142 us (0.26)
  other arithmetic: 156 us -> 0 us
  waiting for transfers between devices: 155 us -> 0 us
  Pallas kernels: 0 us -> 138 us
  matrix products: 103 us -> 0 us
  blocking collectives: 103 us -> 0 us
  between operations: 14 us -> 0.65 us
    all_gather x4 -> x0, waiting for transfers between devices: 153 us -> none  [the longest x3 120 us: joined(): everything = jax.tree.map(lambda part: lax.all_gather(part, axis), array)]
    pallas_call x0 -> x1, Pallas kernels: none -> 138 us  [per_device(): pl.pallas_call(kernel, out_shape=(jax.ShapeDtypeStruct((8, 128), F32), ja...]
    all_gather x5 -> x0, blocking collectives: 103 us -> none  [the longest x4 79.1 us: joined(): everything = jax.tree.map(lambda part: lax.all_gather(part, axis), array)]
    dot_general x9 -> x0, matrix products: 103 us -> none  [the longest x8 71.4 us: map_pass(): jnp.dot(weights, tgt_rows, precision=lax.Precision.HIGHEST, preferred_ele...]
    reduce_sum x26 -> x0, other arithmetic: 79 us -> none  [the longest x8 25.1 us: row_pass(): return (top, jnp.sum(jnp.exp(scores - top[:, None]), axis=1))]
    reduce_max x24 -> x0, other arithmetic: 64.6 us -> none  [the longest x8 21.8 us: column_step(): top = jnp.max(scores, axis=0)]
    add x60 -> x0, other arithmetic: 12.1 us -> none  [the longest x7 10.5 us: map_combine(): first[2] * scale_one[:, None] + second[2] * scale_two[:, None]]
  transfers between devices with their start and end apart: 4 -> 0, of which waited for: 4 -> 0; matrix products, arithmetic and copies ran while one was open for 0% -> 0% of each run, Pallas kernels for 0% -> 0%
where the time goes in v1:
time: 142 us
  Pallas kernels  138 us (97%)
  local copies, waits for them, and re-layouts  3.3 us (2%)
    pallas_call x1, Pallas kernels, per_device(): pl.pallas_call(kernel, out_shape=(jax.ShapeDtypeStruct((8, 128), F32), ja...  138 us
    unnamed x5, local copies, waits for them, and re-layouts  3.3 us

profile of v1, /device:TPU:1, one launch (start us, length us, event | category | flops | bytes accessed | tf_op | source)
XLA Modules:
  0.0 141.8 jit_solution(7472531748737433787)
XLA Ops:
  0.6 137.8 %shard_map.58 = (f32[8,128]{1,0:T(8,128)}, f32[64,128]{1,0:T(8,128)}, f32[128,128]{1,0:T(8,128)}) custom-call(f32[128,128]{1,0:T(8,128)} %src_ref.1, f32[256,128]{1,0:T(8,128)} %tgt_ref.1, f32[64,128]{1,0:T(8,128)} %bitcast.5), custom_call_target="tpu_custom_call" | custom-call | flops 17179869184 | bytes 1048576 | tf_op jit(solution)/shard_map/pallas_call | solution.py:500
  138.4 0.0 copy-start
  138.4 1.3 copy.9
  139.7 1.4 copy.10
  141.1 0.0 copy-done
  141.1 0.6 copy.11
Async XLA Ops:
  138.4 2.7 %copy-start = (f32[128,128]{1,0:T(8,128)S(1)}, f32[128,128]{1,0:T(8,128)}, u32[]{:S(2)}) copy-start(f32[128,128]{1,0:T(8,128)} %get-tuple-element.14) | copy-start | bytes 196612

commit v2 on v1

v2 whole, which is shorter than its diff:
```python
import math

import jax
import jax.numpy as jnp
from jax import lax
from jax.experimental import pallas as pl
from jax.experimental.pallas import tpu as pltpu
from jax.sharding import PartitionSpec as P

epsilon = 0.05
LN2 = math.log(2.0)
ALPHA = 1.0 / (epsilon * LN2)
MESH = pl.DeviceIdType.MESH
F32 = jnp.float32
BF16 = jnp.bfloat16
NSRC = 32
NTGT = 8
WIDE = 4
SIDE = 4
PAIR = 2 * SIDE
LAG = 16
ORDER = (1, 7, 2, 6, 0, 4, 3, 5)
EARLY = 640


STEPS = (
    (0, 0), (1, 0), (3, 0), (2, 0), (0, 1), (0, 3), (1, 1), (1, 3),
    (3, 1), (3, 3), (0, 2), (1, 2), (2, 1), (2, 3), (3, 2), (2, 2),
)
HALVED = (10, 11, 14)


def look_up(m, values):
    found = values[0]
    for k in range(1, len(values)):
        found = jnp.where(m == k, values[k], found)
    return found


def kernel(
    src_ref, tgt_ref, pot_ref, sp_ref, tp_ref, map_ref,
    sbuf, tbuf, lhs, cols, scores, top, total, rslot, rrow, rcol,
    lsend, lrecv, call, colmax, acc, den, zsend, zland,
    z_send, z_recv, p1_send, p2_send, half_send, sib_send, t_recv, sib_recv,
    r_send, r_recv, l_send, l_recv, c_send, c_recv, m_send, m_recv,
):
    me = lax.axis_index("src")
    z = lax.axis_index("tgt")
    core = me % 2
    chip = me // 2
    x = chip % SIDE
    y = chip // SIDE
    sib = me + 1 - 2 * core

    def on_src(i):
        return {"src": i}

    def on_tgt(i):
        return {"tgt": (i + NTGT) % NTGT}

    def rcopy(src, dst, send, recv, dev):
        return pltpu.make_async_remote_copy(
            src_ref=src, dst_ref=dst, send_sem=send, recv_sem=recv, device_id=dev, device_id_type=MESH
        )

    bar = pltpu.get_barrier_semaphore()

    def greet_src(i, carry):
        pl.semaphore_signal(bar, inc=1, device_id=on_src((me + i) % NSRC), device_id_type=MESH)
        return carry

    def greet_tgt(i, carry):
        pl.semaphore_signal(bar, inc=1, device_id=on_tgt(z + i), device_id_type=MESH)
        return carry

    lax.fori_loop(1, NSRC, greet_src, 0)
    lax.fori_loop(1, NTGT, greet_tgt, 0)

    for h in range(2):
        tbuf[chip, core, h] = tgt_ref[pl.ds(h * 128, 128), :]
    sbuf[0] = src_ref[...]

    lane = lax.broadcasted_iota(jnp.int32, (128, 128), 1)
    row = lax.broadcasted_iota(jnp.int32, (128, 128), 0)
    eye = lane == row

    def split3(a):
        a1 = a.astype(BF16).astype(F32)
        rest = a - a1
        a2 = rest.astype(BF16).astype(F32)
        return a1, a2, rest - a2

    def prep_src(place, d):
        s = sbuf[d]
        scaled = s * (2.0 * ALPHA)
        hi = scaled.astype(BF16)
        lo = (scaled - hi.astype(F32)).astype(BF16)
        b1, b2, b3 = split3(-ALPHA * jnp.sum(s * s, axis=1, keepdims=True))
        extra = jnp.where(lane == 0, b1, jnp.where(lane == 1, b2, jnp.where(lane == 2, b3, jnp.where(lane < 6, 1.0, 0.0))))
        rows = pl.ds(place * 128, 128)
        lhs[rows, 0:128] = hi
        lhs[rows, 128:256] = hi
        lhs[rows, 256:384] = lo
        lhs[rows, 384:512] = extra.astype(BF16)

    def prep_tgt(u, q, h):
        for c in range(2):
            t = tbuf[q, c, h]
            pot = pot_ref[pl.ds(q * 4 + c * 2 + h, 1), :]
            hi = t.astype(BF16)
            lo = (t - hi.astype(F32)).astype(BF16)
            a1, a2, a3 = split3(ALPHA * jnp.sum(jnp.where(eye, pot, 0.0) - t * t, axis=1, keepdims=True))
            extra = jnp.where(lane < 3, 1.0, jnp.where(lane == 3, a1, jnp.where(lane == 4, a2, jnp.where(lane == 5, a3, 0.0))))
            rows = pl.ds(c * 128, 128)
            cols[u, rows, 0:128] = lo
            cols[u, rows, 128:256] = hi
            cols[u, rows, 256:384] = hi
            cols[u, rows, 384:512] = extra.astype(BF16)

    prep_src(ORDER.index(0), 0)
    top[...] = jnp.full((1024, 128), -jnp.inf, F32)
    total[...] = jnp.zeros((1024, 128), F32)
    pl.semaphore_wait(bar, NSRC + NTGT - 2)

    def at(xx, yy):
        return (((yy + SIDE) % SIDE) * SIDE + (xx + SIDE) % SIDE) * 2 + core

    def step_of(i):
        return (1, -1, 2)[i]

    def p1_copy(h, i):
        step = step_of(i)
        dev = on_src(at(x + step * (1 - h), y + step * h))
        piece = tbuf.at[chip, core, h]
        return rcopy(piece, piece, p1_send.at[h * 3 + i], t_recv.at[0, h * 16 + chip], dev)

    def z_copy(n):
        up = n % 2 == 0
        sign = 1 if up else -1
        if n < 4:
            d, to, far = 0, (-sign * (1 + n // 2)) % NTGT, 1 + n // 2
        elif n < 6:
            d, to, far = (-2 * sign) % NTGT, (-3 * sign) % NTGT, 1
        else:
            rows = pl.ds(0 if up else 64, 64)
            d = (-2 * sign) % NTGT
            return rcopy(sbuf.at[d, rows], sbuf.at[4, rows], z_send.at[n], z_recv.at[4 if up else 8], on_tgt(z + 2 * sign))
        return rcopy(sbuf.at[d], sbuf.at[to], z_send.at[n], z_recv.at[to], on_tgt(z + far * sign))

    for i in range(3):
        for h in range(2):
            p1_copy(h, i).start()
    for n in (2, 3, 0, 1):
        z_copy(n).start()

    def z_wait(d):
        rcopy(sbuf.at[d], sbuf.at[d], z_send.at[0], z_recv.at[d], on_tgt(z + 1)).wait_recv()

    def z_near():
        for d, n in ((6, 4), (2, 5)):
            z_wait(d)
            z_copy(n).start()
            z_copy(n + 2).start()
        for d in (6, 2):
            prep_src(ORDER.index(d), d)

    def z_next():
        for d in (7, 1):
            z_wait(d)
            prep_src(ORDER.index(d), d)

    def z_late():
        for d in (5, 3):
            z_wait(d)
            prep_src(ORDER.index(d), d)
        for i in range(2):
            part = sbuf.at[4, pl.ds(i * 64, 64)]
            rcopy(part, part, z_send.at[0], z_recv.at[4 + 4 * i], on_tgt(z + 1)).wait_recv()
        prep_src(ORDER.index(4), 4)

    def place_of(m, h):
        code = look_up(m, [a * 4 + b for a, b in STEPS])
        d1 = code // 4
        d2 = code % 4
        dx = (1 - h) * d1 + h * d2
        dy = (1 - h) * d2 + h * d1
        return d2, ((y + dy) % SIDE) * SIDE + (x + dx) % SIDE

    def p2_copy(m, h, q, i):
        step = step_of(i)
        dev = on_src(at(x + step * h, y + step * (1 - h)))
        piece = tbuf.at[q, core, h]
        return rcopy(piece, piece, p2_send.at[m * 6 + h * 3 + i], t_recv.at[0, h * 16 + q], dev)

    def half_copy(m, h, q, d2):
        step = d2 - 2
        part = (3 - d2) // 2
        dev = on_src(at(x + step * h, y + step * (1 - h)))
        piece = tbuf.at[q, core, h, pl.ds(pl.multiple_of(part * 64, 64), 64)]
        return rcopy(piece, piece, half_send.at[(m - 4) * 2 + h], t_recv.at[part, h * 16 + q], dev)

    def sib_copy(m, h, q):
        piece = tbuf.at[q, core, h]
        return rcopy(piece, piece, sib_send.at[m * 2 + h], sib_recv.at[h * 16 + q], on_src(sib))

    def handed_on(m):
        return jnp.logical_and(m >= 4, m < 10)

    def gather_step(m):
        halved = look_up(m, [int(k in HALVED) for k in range(16)])
        for h in range(2):
            d2, q = place_of(m, h)
            piece = tbuf.at[q, core, h]

            @pl.when(jnp.logical_and(m > 0, halved == 0))
            def _():
                rcopy(piece, piece, sib_send.at[0], t_recv.at[0, h * 16 + q], on_src(sib)).wait_recv()

            @pl.when(halved == 1)
            def _():
                for i in range(2):
                    part = tbuf.at[q, core, h, pl.ds(i * 64, 64)]
                    rcopy(part, part, sib_send.at[0], t_recv.at[i, h * 16 + q], on_src(sib)).wait_recv()

            @pl.when(handed_on(m))
            def _():
                half_copy(m, h, q, d2).start()

            @pl.when(m < 4)
            def _():
                for i in range(2):
                    p2_copy(m, h, q, i).start()

            @pl.when(m == 3)
            def _():
                p2_copy(m, h, q, 2).start()

            sib_copy(m, h, q).start()

    def score_rows(m, r0, n):
        us = []
        for h in range(2):
            _, q = place_of(m, h)
            u = q * 2 + h
            us.append(u)
            scores[u, pl.ds(r0, n), :] = lax.dot_general(
                lhs[pl.ds(r0, n), :], cols[u], (((1,), (1,)), ((), ())), preferred_element_type=F32
            )
        for r in range(r0, r0 + n, 64):
            rows = pl.ds(r, 64)
            parts = [scores[u, rows, pl.ds(k * 128, 128)] for u in us for k in range(2)]
            old = top[rows, :]
            new = jnp.maximum(jnp.maximum(parts[0], parts[1]), jnp.maximum(parts[2], parts[3]))
            new = jnp.maximum(old, new)
            e = [jnp.exp2(p - new) for p in parts]
            total[rows, :] = total[rows, :] * jnp.exp2(old - new) + ((e[0] + e[1]) + (e[2] + e[3]))
            top[rows, :] = new

    def first_pass(m, carry):
        @pl.when(m < 16)
        def _():
            gather_step(m)

        for n, action in ((1, z_near), (2, z_next), (10, z_late)):

            @pl.when(m == n)
            def _():
                action()

        p = m - 2

        @pl.when(p >= 0)
        def _():
            for h in range(2):
                _, q = place_of(p, h)
                piece = tbuf.at[q, 1 - core, h]
                rcopy(piece, piece, sib_send.at[0], sib_recv.at[h * 16 + q], on_src(sib)).wait_recv()
                prep_tgt(q * 2 + h, q, h)
            score_rows(p, 0, EARLY)

        @pl.when(p >= PAIR)
        def _():
            def both(i, c):
                score_rows(p - PAIR + PAIR * i, EARLY, 1024 - EARLY)
                return c

            lax.fori_loop(0, 2, both, 0)

        return carry

    lax.fori_loop(0, 18, first_pass, 0)

    for place, d in enumerate(ORDER):
        rows = pl.ds(place * 128, 128)
        m = top[rows, :]
        high = jnp.max(m, axis=1, keepdims=True)
        s = jnp.sum(total[rows, :] * jnp.exp2(m - high), axis=1, keepdims=True)
        r = high + jnp.log2(s)
        rslot[z, pl.ds((z + d) % NTGT, 1), :] = jnp.sum(jnp.where(eye, r, 0.0), axis=0, keepdims=True)

    def r_copy(i):
        return rcopy(rslot.at[z], rslot.at[z], r_send.at[i], r_recv.at[z], on_tgt(z + i))

    for i in range(1, NTGT):
        r_copy(i).start()

    for h in range(2):
        for i in range(3):
            p1_copy(h, i).wait_send()
    for n in range(8):
        z_copy(n).wait_send()

    def gather_sent(m, carry):
        for h in range(2):
            d2, q = place_of(m, h)

            @pl.when(handed_on(m))
            def _():
                half_copy(m, h, q, d2).wait_send()

            @pl.when(m < 4)
            def _():
                for i in range(2):
                    p2_copy(m, h, q, i).wait_send()

            @pl.when(m == 3)
            def _():
                p2_copy(m, h, q, 2).wait_send()

            sib_copy(m, h, q).wait_send()
        return carry

    lax.fori_loop(0, 16, gather_sent, 0)

    for i in range(1, NTGT):
        other = (z + i) % NTGT
        slot = rslot.at[other]
        rcopy(slot, slot, r_send.at[0], r_recv.at[other], on_tgt(z + i)).wait_recv()
    slots = [rslot[i] for i in range(NTGT)]
    high = slots[0]
    for s in slots[1:]:
        high = jnp.maximum(high, s)
    sums = jnp.exp2(slots[0] - high)
    for s in slots[1:]:
        sums = sums + jnp.exp2(s - high)
    r_all = high + jnp.log2(sums)
    rrow[...] = r_all
    sp_ref[...] = -epsilon * math.log(NSRC * 1024) - (epsilon * LN2) * r_all
    for place, d in enumerate(ORDER):
        one = rrow[pl.ds((z + d) % NTGT, 1), :]
        rcol[pl.ds(place * 128, 128), :] = jnp.transpose(jnp.broadcast_to(one, (128, 128)))

    def l_copy(u):
        return rcopy(lsend.at[u], lrecv.at[me], l_send.at[u], l_recv.at[me], on_src(u))

    def c_copy(i):
        return rcopy(call.at[me], call.at[me], c_send.at[i], c_recv.at[me], on_src((me + i) % NSRC))

    def column_unit(u):
        for k in range(2):
            lanes = pl.ds(k * 128, 128)
            tops, sums = [], []
            for b in range(8):
                rows = pl.ds(b * 128, 128)
                v = scores[u, rows, lanes] - rcol[rows, :]
                q = jnp.max(v, axis=0, keepdims=True)
                e = jnp.exp2(v - q)
                scores[u, rows, lanes] = e
                tops.append(q)
                sums.append(jnp.sum(e, axis=0, keepdims=True))
            tops = jnp.concatenate(tops, axis=0)
            sums = jnp.concatenate(sums, axis=0)
            colmax[u, :, lanes] = tops
            high = jnp.max(tops, axis=0, keepdims=True)
            lsend[u, :, lanes] = high + jnp.log2(jnp.sum(sums * jnp.exp2(tops - high), axis=0, keepdims=True))

        @pl.when(u != me)
        def _():
            l_copy(u).start()

        @pl.when(u == me)
        def _():
            lrecv[me] = lsend[u]

    def column_total():
        def arrived(i, carry):
            other = (me + i) % NSRC
            slot = lrecv.at[other]
            rcopy(slot, slot, l_send.at[0], l_recv.at[other], on_src(other)).wait_recv()
            return carry

        lax.fori_loop(1, NSRC, arrived, 0)
        parts = lrecv[...]
        high = jnp.max(parts, axis=0)
        call[me] = high + jnp.log2(jnp.sum(jnp.exp2(parts - high[None]), axis=0))

        def tell(i, carry):
            c_copy(i).start()
            return carry

        lax.fori_loop(1, NSRC, tell, 0)

    def second_pass(k, carry):
        column_unit(k)

        @pl.when(k == me + LAG)
        def _():
            column_total()

        return carry

    lax.fori_loop(0, NSRC, second_pass, 0)

    @pl.when(me + LAG >= NSRC)
    def _():
        column_total()

    acc[...] = jnp.zeros((1024, 256), F32)
    den[...] = jnp.zeros((1024, 128), F32)

    def map_units(i, r0, n, wait):
        if wait:
            for j in range(WIDE):
                u = i * WIDE + j

                @pl.when(u != me)
                def _():
                    slot = call.at[u]
                    rcopy(slot, slot, c_send.at[0], c_recv.at[u], on_src(u)).wait_recv()

        high, low, t, sums = [], [], [], None
        for j in range(WIDE):
            u = i * WIDE + j
            f = jnp.exp2(colmax[u] - call[u])
            ws = [scores[u, pl.ds(b * 128, 128), :] * f[b : b + 1, :] for b in range(r0 // 128, (r0 + n) // 128)]
            w = jnp.concatenate(ws, axis=0)
            half = w[:, :128] + w[:, 128:]
            sums = half if sums is None else sums + half
            hi = w.astype(BF16)
            high.append(hi)
            low.append((w - hi.astype(F32)).astype(BF16))
            t.append(cols[u, :, 0:256])
        rows = pl.ds(r0, n)
        den[rows, :] += sums
        acc[rows, :] += jnp.dot(
            jnp.concatenate(high + low, axis=1), jnp.concatenate(t + t, axis=0), preferred_element_type=F32
        )

    def map_rows(first, last, r0, n, wait):
        def body(i, carry):
            map_units(i, r0, n, wait)
            return carry

        lax.fori_loop(first // WIDE, last // WIDE, body, 0)

    def block(place):
        rows = pl.ds(place * 128, 128)
        d = jnp.sum(den[rows, :], axis=1, keepdims=True)
        return acc[rows, 0:128] + acc[rows, 128:256], jnp.sum(jnp.where(eye, d, 0.0), axis=0, keepdims=True)

    def z_sum(n):
        sign = 1 if n % 2 == 0 else -1
        rows = pl.ds(0, 136) if n >= 2 else (pl.ds(0, 64) if n == 0 else pl.ds(64, 72))
        far = (2, 1, 2, 1)[n // 2]
        return rcopy(zsend.at[n, rows], zland.at[n, rows], m_send.at[n], m_recv.at[n], on_tgt(z + far * sign))

    def put(n, place):
        num, d = block(place)
        zsend[n, 0:128, :] = num
        zsend[n, 128:136, :] = jnp.broadcast_to(d, (8, 128))

    map_rows(0, LAG, 0, 1024, True)
    map_rows(LAG, NSRC, EARLY, 1024 - EARLY, True)
    for n, d in ((0, 4), (1, 4), (2, 3), (3, 5)):
        put(n, ORDER.index(d))
        z_sum(n).start()
    map_rows(LAG, NSRC, 0, EARLY, False)
    for n, d in ((6, 1), (7, 7)):
        put(n, ORDER.index(d))
        z_sum(n).start()
    for n, d in ((4, 2), (5, 6)):
        put(n, ORDER.index(d))
        for k in (n - 4, n - 2):
            z_sum(k).wait_recv()
        zsend[n] += zland[n - 2]
        part = pl.ds(0, 64) if n == 4 else pl.ds(64, 72)
        zsend[n, part, :] += zland[n - 4, part, :]
        z_sum(n).start()
    own_num, own_den = block(ORDER.index(0))

    for u in range(NSRC):
        for c in range(2):
            r = (u // 2) * 4 + c * 2 + u % 2
            tp_ref[r : r + 1, :] = (
                pot_ref[r : r + 1, :] - (epsilon * LN2) * call[u, :, c * 128 : (c + 1) * 128]
                - epsilon * math.log(NTGT * 8192 / (NSRC * 1024))
            )
    for i in range(1, NTGT):
        r_copy(i).wait_send()

    def small_sent(i, carry):
        c_copy(i).wait_send()
        l_copy((me + i) % NSRC).wait_send()
        return carry

    lax.fori_loop(1, NSRC, small_sent, 0)
    for n in range(8):
        z_sum(n).wait_send()
    for n in range(4, 8):
        z_sum(n).wait_recv()
    num = (own_num + (zland[6, 0:128, :] + zland[7, 0:128, :])) + (zland[4, 0:128, :] + zland[5, 0:128, :])
    d = (own_den + (zland[6, 128:129, :] + zland[7, 128:129, :])) + (zland[4, 128:129, :] + zland[5, 128:129, :])
    d = jnp.sum(jnp.where(eye, d, 0.0), axis=1, keepdims=True)
    map_ref[...] = num / d


def finish(sp, tp, mapped, sp_ref, tp_ref, map_ref):
    sp_ref[...] = sp[...]
    tp_ref[...] = tp[...]
    map_ref[...] = mapped[...]


def per_device(sources, targets, potential_in):
    vmem = pl.BlockSpec(memory_space=pltpu.VMEM)
    dma = pltpu.SemaphoreType.DMA
    shapes = (
        jax.ShapeDtypeStruct((8, 128), F32),
        jax.ShapeDtypeStruct((64, 128), F32),
        jax.ShapeDtypeStruct((128, 128), F32),
    )
    results = pl.pallas_call(
        kernel,
        out_shape=shapes,
        in_specs=[vmem] * 3,
        out_specs=(vmem,) * 3,
        scratch_shapes=[
            pltpu.VMEM((8, 128, 128), F32),
            pltpu.VMEM((16, 2, 2, 128, 128), F32),
            pltpu.VMEM((1024, 512), BF16),
            pltpu.VMEM((32, 256, 512), BF16),
            pltpu.VMEM((32, 1024, 256), F32),
            pltpu.VMEM((1024, 128), F32),
            pltpu.VMEM((1024, 128), F32),
            pltpu.VMEM((8, 8, 128), F32),
            pltpu.VMEM((8, 128), F32),
            pltpu.VMEM((1024, 128), F32),
            pltpu.VMEM((32, 1, 256), F32),
            pltpu.VMEM((32, 1, 256), F32),
            pltpu.VMEM((32, 1, 256), F32),
            pltpu.VMEM((32, 8, 256), F32),
            pltpu.VMEM((1024, 256), F32),
            pltpu.VMEM((1024, 128), F32),
            pltpu.VMEM((8, 136, 128), F32),
            pltpu.VMEM((8, 136, 128), F32),
            dma((8,)),
            dma((9,)),
            dma((6,)),
            dma((24,)),
            dma((12,)),
            dma((32,)),
            dma((2, 32)),
            dma((32,)),
            dma((8,)),
            dma((8,)),
            dma((32,)),
            dma((32,)),
            dma((32,)),
            dma((32,)),
            dma((8,)),
            dma((8,)),
        ],
        compiler_params=pltpu.CompilerParams(
            collective_id=0, has_side_effects=True, vmem_limit_bytes=62 * 1024 * 1024
        ),
        cost_estimate=pl.CostEstimate(
            flops=2 * 1024 * 8192 * 1024, bytes_accessed=1 << 20, transcendentals=2 * 1024 * 8192
        ),
    )(sources, targets, potential_in.reshape(64, 128))
    sp, tp, mapped = pl.pallas_call(
        finish, out_shape=shapes, in_specs=[vmem] * 3, out_specs=(vmem,) * 3
    )(*results)
    return sp.reshape(1024), tp.reshape(8192), mapped


def solution(mesh):
    return jax.shard_map(
        per_device,
        mesh=mesh,
        in_specs=(P(("src", "tgt"), None), P(("tgt", "src"), None), P("tgt")),
        out_specs=(P("src"), P("tgt"), P(("src", "tgt"), None)),
        check_vma=False,
    )
```

time: 142 us -> 89.9 us (0.63)
  Pallas kernels: 138 us -> 88.6 us
  local copies, waits for them, and re-layouts: 3.3 us -> 0 us
    pallas_call x1 -> x2, Pallas kernels: 138 us -> 88.6 us  [the longest x1 87.1 us: per_device(): pl.pallas_call(kernel, out_shape=shapes, in_specs=[vmem] * 3, out_specs=(...]
    unnamed x5 -> x0, local copies, waits for them, and re-layouts: 3.3 us -> none
where the time goes in v2:
time: 89.9 us; the launch traced here: 89.2 us
  Pallas kernels  88.6 us (99%)
    pallas_call x1, Pallas kernels, per_device(): pl.pallas_call(kernel, out_shape=shapes, in_specs=[vmem] * 3, out_specs=(...  87.1 us

profile of v2, /device:TPU:1, one launch (start us, length us, event | category | flops | bytes accessed | tf_op | source)
XLA Modules:
  0.0 89.2 jit_solution(5466782366663607907)
XLA Ops:
  0.6 87.1 %shard_map.58 = (f32[8,128]{1,0:T(8,128)}, f32[64,128]{1,0:T(8,128)}, f32[128,128]{1,0:T(8,128)}) custom-call(f32[128,128]{1,0:T(8,128)} %src_ref.1, f32[256,128]{1,0:T(8,128)} %tgt_ref.1, f32[64,128]{1,0:T(8,128)} %bitcast.3), custom_call_target="tpu_custom_call" | custom-call | flops 17179869184 | bytes 1048576 | tf_op jit(solution)/shard_map/pallas_call | solution.py:531
  87.7 1.5 %shard_map.59 = (f32[8,128]{1,0:T(8,128)}, f32[64,128]{1,0:T(8,128)}, f32[128,128]{1,0:T(8,128)}) custom-call(f32[8,128]{1,0:T(8,128)} %get-tuple-element.9.sp, f32[64,128]{1,0:T(8,128)} %get-tuple-element.10.tp, f32[128,128]{1,0:T(8,128)} %get-tuple-element.11.mapped), custom_call_target="tpu_custom_call" | custom-call | tf_op jit(solution)/shard_map/pallas_call | solution.py:579

commit v3 on v2

v3 whole, which is shorter than its diff:
```python
import math

import jax
import jax.numpy as jnp
from jax import lax
from jax.experimental import pallas as pl
from jax.experimental.pallas import tpu as pltpu
from jax.sharding import PartitionSpec as P

epsilon = 0.05
LN2 = math.log(2.0)
ALPHA = 1.0 / (epsilon * LN2)
MESH = pl.DeviceIdType.MESH
F32 = jnp.float32
BF16 = jnp.bfloat16
NSRC = 32
NTGT = 8
ORDER = (4, 3, 5, 1, 7, 0, 2, 6)
SIDE = 4
WIDE = 8
AHEAD = 2
EARLY = 5


def gray(i):
    return i + i // 2 - 2 * (i // 3)


def kernel(
    src_ref, tgt_ref, pot_ref, sp_ref, tp_ref, map_ref,
    sbuf, tbuf, lhs, cols, scores, top, total, rslot, rcol,
    lsend, lrecv, call, colmax, acc, den, zsend, zland, colsum,
    z_send, z_recv, p1_send, p2_send, sib_send, t_recv, sib_recv,
    r_send, r_recv, l_send, l_recv, c_send, c_recv, m_send, m_recv,
):
    me = lax.axis_index("src")
    z = lax.axis_index("tgt")
    core = me % 2
    chip = me // 2
    x = chip % SIDE
    y = chip // SIDE
    sib = me + 1 - 2 * core

    def on_src(i):
        return {"src": i}

    def on_tgt(i):
        return {"tgt": (i + NTGT) % NTGT}

    def rcopy(src, dst, send, recv, dev):
        return pltpu.make_async_remote_copy(
            src_ref=src, dst_ref=dst, send_sem=send, recv_sem=recv, device_id=dev, device_id_type=MESH
        )

    bar = pltpu.get_barrier_semaphore()

    def greet_src(i, carry):
        pl.semaphore_signal(bar, inc=1, device_id=on_src((me + i) % NSRC), device_id_type=MESH)
        return carry

    def greet_tgt(i, carry):
        pl.semaphore_signal(bar, inc=1, device_id=on_tgt(z + i), device_id_type=MESH)
        return carry

    lax.fori_loop(1, NSRC, greet_src, 0)
    lax.fori_loop(1, NTGT, greet_tgt, 0)

    for h in range(2):
        tbuf[chip, core, h] = tgt_ref[pl.ds(h * 128, 128), :]
    sbuf[0] = src_ref[...]

    lane = lax.broadcasted_iota(jnp.int32, (128, 128), 1)
    row = lax.broadcasted_iota(jnp.int32, (128, 128), 0)
    eye = lane == row

    def split3(a):
        a1 = a.astype(BF16).astype(F32)
        rest = a - a1
        a2 = rest.astype(BF16).astype(F32)
        return a1, a2, rest - a2

    def prep_src(d):
        s = sbuf[d]
        scaled = s * (2.0 * ALPHA)
        hi = scaled.astype(BF16)
        lo = (scaled - hi.astype(F32)).astype(BF16)
        b1, b2, b3 = split3(-ALPHA * jnp.sum(s * s, axis=1, keepdims=True))
        extra = jnp.where(lane == 0, b1, jnp.where(lane == 1, b2, jnp.where(lane == 2, b3, jnp.where(lane < 6, 1.0, 0.0))))
        rows = pl.ds(pl.multiple_of((z + d) % NTGT * 128, 128), 128)
        lhs[rows, 0:128] = hi
        lhs[rows, 128:256] = hi
        lhs[rows, 256:384] = lo
        lhs[rows, 384:512] = extra.astype(BF16)

    def prep_tgt(u, q, h):
        for c in range(2):
            t = tbuf[q, c, h]
            pot = pot_ref[pl.ds(q * 4 + c * 2 + h, 1), :]
            hi = t.astype(BF16)
            lo = (t - hi.astype(F32)).astype(BF16)
            a1, a2, a3 = split3(ALPHA * jnp.sum(jnp.where(eye, pot, 0.0) - t * t, axis=1, keepdims=True))
            extra = jnp.where(lane < 3, 1.0, jnp.where(lane == 3, a1, jnp.where(lane == 4, a2, jnp.where(lane == 5, a3, 0.0))))
            rows = pl.ds(c * 128, 128)
            cols[u, rows, 0:128] = lo
            cols[u, rows, 128:256] = hi
            cols[u, rows, 256:384] = hi
            cols[u, rows, 384:512] = extra.astype(BF16)

    prep_src(0)
    top[...] = jnp.full((1024, 128), -jnp.inf, F32)
    total[...] = jnp.zeros((1024, 128), F32)
    pl.semaphore_wait(bar, NSRC + NTGT - 2)

    def at(xx, yy):
        return (((yy + SIDE) % SIDE) * SIDE + (xx + SIDE) % SIDE) * 2 + core

    def step_of(i):
        return (1, -1, 2)[i]

    def p1_copy(h, i):
        step = step_of(i)
        dev = on_src(at(x + step * (1 - h), y + step * h))
        piece = tbuf.at[chip, core, h]
        return rcopy(piece, piece, p1_send.at[h * 3 + i], t_recv.at[h * 16 + chip], dev)

    def z_copy(n):
        up = n % 2 == 0
        sign = 1 if up else -1
        if n < 4:
            d, to, far = 0, (-sign * (1 + n // 2)) % NTGT, 1 + n // 2
        elif n < 6:
            d, to, far = (-2 * sign) % NTGT, (-3 * sign) % NTGT, 1
        else:
            rows = pl.ds(0 if up else 64, 64)
            d = (-2 * sign) % NTGT
            return rcopy(sbuf.at[d, rows], sbuf.at[4, rows], z_send.at[n], z_recv.at[4 if up else 8], on_tgt(z + 2 * sign))
        return rcopy(sbuf.at[d], sbuf.at[to], z_send.at[n], z_recv.at[to], on_tgt(z + far * sign))

    for i in range(3):
        for h in range(2):
            p1_copy(h, i).start()
    for n in (2, 3, 0, 1):
        z_copy(n).start()

    def z_wait(d):
        rcopy(sbuf.at[d], sbuf.at[d], z_send.at[0], z_recv.at[d], on_tgt(z + 1)).wait_recv()

    def z_near():
        for d, n in ((6, 4), (2, 5)):
            z_wait(d)
            z_copy(n).start()
            z_copy(n + 2).start()
        for d in (6, 2):
            prep_src(d)

    def z_next():
        for d in (7, 1):
            z_wait(d)
            prep_src(d)

    def z_late():
        for d in (5, 3):
            z_wait(d)
            prep_src(d)
        for i in range(2):
            part = sbuf.at[4, pl.ds(i * 64, 64)]
            rcopy(part, part, z_send.at[0], z_recv.at[4 + 4 * i], on_tgt(z + 1)).wait_recv()
        prep_src(4)

    def place_of(m, h):
        g1 = jnp.where(m < 4, m, (m + 8) // 3 - 4)
        g2 = jnp.where(m < 4, 0, (m + 8) % 3 + 1)
        d1, d2 = gray(g1), gray(g2)
        dx = (1 - h) * d1 + h * d2
        dy = (1 - h) * d2 + h * d1
        return ((y + dy) % SIDE) * SIDE + (x + dx) % SIDE

    def slot_of(u):
        q, h = u // 2, u % 2
        dx = (q % SIDE - x + SIDE) % SIDE
        dy = (q // SIDE - y + SIDE) % SIDE
        g1 = gray(jnp.where(h == 0, dx, dy))
        g2 = gray(jnp.where(h == 0, dy, dx))
        return 2 * jnp.where(g2 == 0, g1, 3 + 3 * g1 + g2) + h

    def p2_copy(m, h, q, i):
        step = step_of(i)
        dev = on_src(at(x + step * h, y + step * (1 - h)))
        piece = tbuf.at[q, core, h]
        return rcopy(piece, piece, p2_send.at[m * 6 + h * 3 + i], t_recv.at[h * 16 + q], dev)

    def sib_copy(m, h, q):
        piece = tbuf.at[q, core, h]
        return rcopy(piece, piece, sib_send.at[m * 2 + h], sib_recv.at[h * 16 + q], on_src(sib))

    def gather_step(m):
        for h in range(2):
            q = place_of(m, h)
            piece = tbuf.at[q, core, h]

            @pl.when(m > 0)
            def _():
                rcopy(piece, piece, sib_send.at[0], t_recv.at[h * 16 + q], on_src(sib)).wait_recv()

            @pl.when(m < 4)
            def _():
                for i in range(3):
                    p2_copy(m, h, q, i).start()

            sib_copy(m, h, q).start()

    def score_rows(us, r0, n):
        for u in us:
            scores[u, pl.ds(r0, n), :] = lax.dot_general(
                lhs[pl.ds(r0, n), :], cols[u], (((1,), (1,)), ((), ())), preferred_element_type=F32
            )
        for r in range(r0, r0 + n, 64):
            rows = pl.ds(r, 64)
            parts = [scores[u, rows, pl.ds(k * 128, 128)] for u in us for k in range(2)]
            old = top[rows, :]
            new = old
            for p in parts:
                new = jnp.maximum(new, p)
            sums = total[rows, :] * jnp.exp2(old - new)
            for p in parts:
                sums = sums + jnp.exp2(p - new)
            total[rows, :] = sums
            top[rows, :] = new

    def lead(m, carry):
        gather_step(m)

        @pl.when(m == 2)
        def _():
            z_near()

        return carry

    lax.fori_loop(0, 4, lead, 0)
    z_next()
    z_late()

    def first_pass(p, carry):
        m = p + AHEAD

        @pl.when(jnp.logical_and(m >= 4, m < 16))
        def _():
            gather_step(m)

        for h in range(2):
            q = place_of(p, h)
            piece = tbuf.at[q, 1 - core, h]
            rcopy(piece, piece, sib_send.at[0], sib_recv.at[h * 16 + q], on_src(sib)).wait_recv()
        for h in range(2):
            prep_tgt(p * 2 + h, place_of(p, h), h)
        score_rows((p * 2, p * 2 + 1), 0, EARLY * 128)
        return carry

    lax.fori_loop(0, 16, first_pass, 0)

    def r_copy(part, i):
        slot = rslot.at[part, z]
        return rcopy(slot, slot, r_send.at[part * NTGT + i], r_recv.at[part * NTGT + z], on_tgt(z + i))

    def row_sums(part, blocks):
        rslot[part, z] = jnp.zeros((8, 128), F32)
        for c in blocks:
            rows = pl.ds(c * 128, 128)
            m = top[rows, :]
            high = jnp.max(m, axis=1, keepdims=True)
            s = jnp.sum(total[rows, :] * jnp.exp2(m - high), axis=1, keepdims=True)
            r = high + jnp.log2(s)
            rslot[part, z, c : c + 1, :] = jnp.sum(jnp.where(eye, r, 0.0), axis=0, keepdims=True)
        for i in range(1, NTGT):
            r_copy(part, i).start()

    def row_totals(part, blocks):
        for i in range(1, NTGT):
            other = (z + i) % NTGT
            slot = rslot.at[part, other]
            rcopy(slot, slot, r_send.at[0], r_recv.at[part * NTGT + other], on_tgt(z + i)).wait_recv()
        slots = [rslot[part, i] for i in range(NTGT)]
        high = slots[0]
        for s in slots[1:]:
            high = jnp.maximum(high, s)
        sums = jnp.exp2(slots[0] - high)
        for s in slots[1:]:
            sums = sums + jnp.exp2(s - high)
        r_all = high + jnp.log2(sums)
        for c in blocks:
            one = r_all[c : c + 1, :]
            sp_ref[c : c + 1, :] = -epsilon * math.log(NSRC * 1024) - (epsilon * LN2) * one
            rcol[pl.ds(c * 128, 128), :] = jnp.transpose(jnp.broadcast_to(one, (128, 128)))

    early, late = range(EARLY), range(EARLY, 8)
    row_sums(0, early)

    def late_rows(i, carry):
        score_rows([i * 4 + j for j in range(4)], EARLY * 128, 1024 - EARLY * 128)
        return carry

    lax.fori_loop(0, 8, late_rows, 0)
    row_sums(1, late)

    for h in range(2):
        for i in range(3):
            p1_copy(h, i).wait_send()
    for n in range(8):
        z_copy(n).wait_send()

    def gather_sent(m, carry):
        for h in range(2):
            q = place_of(m, h)

            @pl.when(m < 4)
            def _():
                for i in range(3):
                    p2_copy(m, h, q, i).wait_send()

            sib_copy(m, h, q).wait_send()
        return carry

    lax.fori_loop(0, 16, gather_sent, 0)
    row_totals(0, early)

    def l_copy(u):
        return rcopy(lsend.at[u], lrecv.at[me], l_send.at[u], l_recv.at[me], on_src(u))

    def c_copy(i):
        return rcopy(call.at[me], call.at[me], c_send.at[i], c_recv.at[me], on_src((me + i) % NSRC))

    def column_blocks(slot, blocks):
        b0, n = blocks[0], len(blocks)
        for k in range(2):
            lanes = pl.ds(k * 128, 128)
            tops, sums = [], []
            for b in blocks:
                rows = pl.ds(b * 128, 128)
                v = scores[slot, rows, lanes] - rcol[rows, :]
                q = jnp.max(v, axis=0, keepdims=True)
                e = jnp.exp2(v - q)
                scores[slot, rows, lanes] = e
                tops.append(q)
                sums.append(jnp.sum(e, axis=0, keepdims=True))
            colmax[slot, pl.ds(b0, n), lanes] = jnp.concatenate(tops, axis=0)
            colsum[slot, pl.ds(b0, n), lanes] = jnp.concatenate(sums, axis=0)

    def early_blocks(slot, carry):
        column_blocks(slot, early)
        return carry

    def late_blocks(u, carry):
        slot = slot_of(u)
        column_blocks(slot, late)
        tops = colmax[slot]
        high = jnp.max(tops, axis=0, keepdims=True)
        lsend[u] = high + jnp.log2(jnp.sum(colsum[slot] * jnp.exp2(tops - high), axis=0, keepdims=True))

        @pl.when(u != me)
        def _():
            l_copy(u).start()

        @pl.when(u == me)
        def _():
            lrecv[me] = lsend[u]

        return carry

    def column_total():
        def arrived(i, carry):
            other = (me + i) % NSRC
            slot = lrecv.at[other]
            rcopy(slot, slot, l_send.at[0], l_recv.at[other], on_src(other)).wait_recv()
            return carry

        lax.fori_loop(1, NSRC, arrived, 0)
        parts = lrecv[...]
        high = jnp.max(parts, axis=0)
        call[me] = high + jnp.log2(jnp.sum(jnp.exp2(parts - high[None]), axis=0))

        def tell(i, carry):
            c_copy(i).start()
            return carry

        lax.fori_loop(1, NSRC, tell, 0)

    lax.fori_loop(0, NSRC, early_blocks, 0)
    row_totals(1, late)
    lax.fori_loop(0, NSRC, late_blocks, 0)
    column_total()

    acc[...] = jnp.zeros((1024, 256), F32)
    den[...] = jnp.zeros((1024, 128), F32)

    def map_units(i, dists, wait):
        if wait:
            for j in range(WIDE):
                u = i * WIDE + j

                @pl.when(u != me)
                def _():
                    slot = call.at[u]
                    rcopy(slot, slot, c_send.at[0], c_recv.at[u], on_src(u)).wait_recv()

        high, low, t, sums = [], [], [], None
        for j in range(WIDE):
            u = i * WIDE + j
            slot = slot_of(u)
            ws = []
            for d in dists:
                c = (z + d) % NTGT
                f = jnp.exp2(colmax[slot, pl.ds(c, 1), :] - call[u])
                ws.append(scores[slot, pl.ds(pl.multiple_of(c * 128, 128), 128), :] * f)
            w = jnp.concatenate(ws, axis=0)
            half = w[:, :128] + w[:, 128:]
            sums = half if sums is None else sums + half
            hi = w.astype(BF16)
            high.append(hi)
            low.append((w - hi.astype(F32)).astype(BF16))
            t.append(cols[slot, :, 0:256])
        rows = pl.ds(ORDER.index(dists[0]) * 128, len(dists) * 128)
        den[rows, :] += sums
        acc[rows, :] += jnp.dot(
            jnp.concatenate(high + low, axis=1), jnp.concatenate(t + t, axis=0), preferred_element_type=F32
        )

    def map_rows(dists, wait):
        def body(i, carry):
            map_units(i, dists, wait)
            return carry

        lax.fori_loop(0, NSRC // WIDE, body, 0)

    def block(place):
        rows = pl.ds(place * 128, 128)
        d = jnp.sum(den[rows, :], axis=1, keepdims=True)
        return acc[rows, 0:128] + acc[rows, 128:256], jnp.sum(jnp.where(eye, d, 0.0), axis=0, keepdims=True)

    def z_sum(n):
        sign = 1 if n % 2 == 0 else -1
        rows = pl.ds(0, 136) if n >= 2 else (pl.ds(0, 64) if n == 0 else pl.ds(64, 72))
        far = (2, 1, 2, 1)[n // 2]
        return rcopy(zsend.at[n, rows], zland.at[n, rows], m_send.at[n], m_recv.at[n], on_tgt(z + far * sign))

    def put(n, place):
        num, d = block(place)
        zsend[n, 0:128, :] = num
        zsend[n, 128:136, :] = jnp.broadcast_to(d, (8, 128))

    map_rows(ORDER[0:3], True)
    for n, d in ((0, 4), (1, 4), (2, 3), (3, 5)):
        put(n, ORDER.index(d))
        z_sum(n).start()
    map_rows(ORDER[3:6], False)
    for n, d in ((6, 1), (7, 7)):
        put(n, ORDER.index(d))
        z_sum(n).start()
    map_rows(ORDER[6:8], False)
    for n, d in ((4, 2), (5, 6)):
        put(n, ORDER.index(d))
        for k in (n - 4, n - 2):
            z_sum(k).wait_recv()
        zsend[n] += zland[n - 2]
        part = pl.ds(0, 64) if n == 4 else pl.ds(64, 72)
        zsend[n, part, :] += zland[n - 4, part, :]
        z_sum(n).start()
    own_num, own_den = block(ORDER.index(0))

    for u in range(NSRC):
        for c in range(2):
            r = (u // 2) * 4 + c * 2 + u % 2
            tp_ref[r : r + 1, :] = (
                pot_ref[r : r + 1, :] - (epsilon * LN2) * call[u, :, c * 128 : (c + 1) * 128]
                - epsilon * math.log(NTGT * 8192 / (NSRC * 1024))
            )
    for i in range(1, NTGT):
        for part in range(2):
            r_copy(part, i).wait_send()

    def small_sent(i, carry):
        c_copy(i).wait_send()
        l_copy((me + i) % NSRC).wait_send()
        return carry

    lax.fori_loop(1, NSRC, small_sent, 0)
    for n in range(8):
        z_sum(n).wait_send()
    for n in range(4, 8):
        z_sum(n).wait_recv()
    num = (own_num + (zland[6, 0:128, :] + zland[7, 0:128, :])) + (zland[4, 0:128, :] + zland[5, 0:128, :])
    d = (own_den + (zland[6, 128:129, :] + zland[7, 128:129, :])) + (zland[4, 128:129, :] + zland[5, 128:129, :])
    d = jnp.sum(jnp.where(eye, d, 0.0), axis=1, keepdims=True)
    map_ref[...] = num / d


def finish(sp, tp, mapped, sp_ref, tp_ref, map_ref):
    sp_ref[...] = sp[...]
    tp_ref[...] = tp[...]
    map_ref[...] = mapped[...]


def per_device(sources, targets, potential_in):
    vmem = pl.BlockSpec(memory_space=pltpu.VMEM)
    dma = pltpu.SemaphoreType.DMA
    shapes = (
        jax.ShapeDtypeStruct((8, 128), F32),
        jax.ShapeDtypeStruct((64, 128), F32),
        jax.ShapeDtypeStruct((128, 128), F32),
    )
    results = pl.pallas_call(
        kernel,
        out_shape=shapes,
        in_specs=[vmem] * 3,
        out_specs=(vmem,) * 3,
        scratch_shapes=[
            pltpu.VMEM((8, 128, 128), F32),
            pltpu.VMEM((16, 2, 2, 128, 128), F32),
            pltpu.VMEM((1024, 512), BF16),
            pltpu.VMEM((32, 256, 512), BF16),
            pltpu.VMEM((32, 1024, 256), F32),
            pltpu.VMEM((1024, 128), F32),
            pltpu.VMEM((1024, 128), F32),
            pltpu.VMEM((2, 8, 8, 128), F32),
            pltpu.VMEM((1024, 128), F32),
            pltpu.VMEM((32, 1, 256), F32),
            pltpu.VMEM((32, 1, 256), F32),
            pltpu.VMEM((32, 1, 256), F32),
            pltpu.VMEM((32, 8, 256), F32),
            pltpu.VMEM((1024, 256), F32),
            pltpu.VMEM((1024, 128), F32),
            pltpu.VMEM((8, 136, 128), F32),
            pltpu.VMEM((8, 136, 128), F32),
            pltpu.VMEM((32, 8, 256), F32),
            dma((8,)),
            dma((9,)),
            dma((6,)),
            dma((24,)),
            dma((32,)),
            dma((32,)),
            dma((32,)),
            dma((16,)),
            dma((16,)),
            dma((32,)),
            dma((32,)),
            dma((32,)),
            dma((32,)),
            dma((8,)),
            dma((8,)),
        ],
        compiler_params=pltpu.CompilerParams(
            collective_id=0, has_side_effects=True, vmem_limit_bytes=62 * 1024 * 1024
        ),
        cost_estimate=pl.CostEstimate(
            flops=2 * 1024 * 8192 * 1024, bytes_accessed=1 << 20, transcendentals=2 * 1024 * 8192
        ),
    )(sources, targets, potential_in.reshape(64, 128))
    sp, tp, mapped = pl.pallas_call(
        finish, out_shape=shapes, in_specs=[vmem] * 3, out_specs=(vmem,) * 3
    )(*results)
    return sp.reshape(1024), tp.reshape(8192), mapped


def solution(mesh):
    return jax.shard_map(
        per_device,
        mesh=mesh,
        in_specs=(P(("src", "tgt"), None), P(("tgt", "src"), None), P("tgt")),
        out_specs=(P("src"), P("tgt"), P(("src", "tgt"), None)),
        check_vma=False,
    )
```

time: 89.9 us -> 83 us (0.923)
  Pallas kernels: 88.6 us -> 82.2 us
    pallas_call x1, Pallas kernels: 87.1 us -> 80.7 us  [per_device(): pl.pallas_call(kernel, out_shape=shapes, in_specs=[vmem] * 3, out_specs=(...]
where the time goes in v3:
time: 83 us; the launch traced here: 82.8 us
  Pallas kernels  82.2 us (99%)
    pallas_call x1, Pallas kernels, per_device(): pl.pallas_call(kernel, out_shape=shapes, in_specs=[vmem] * 3, out_specs=(...  80.7 us

profile of v3, /device:TPU:1, one launch (start us, length us, event | category | flops | bytes accessed | tf_op | source)
XLA Modules:
  0.0 82.8 jit_solution(11210140748811037048)
XLA Ops:
  0.6 80.7 %shard_map.58 = (f32[8,128]{1,0:T(8,128)}, f32[64,128]{1,0:T(8,128)}, f32[128,128]{1,0:T(8,128)}) custom-call(f32[128,128]{1,0:T(8,128)} %src_ref.1, f32[256,128]{1,0:T(8,128)} %tgt_ref.1, f32[64,128]{1,0:T(8,128)} %bitcast.3), custom_call_target="tpu_custom_call" | custom-call | flops 17179869184 | bytes 1048576 | tf_op jit(solution)/shard_map/pallas_call | solution.py:510
  81.3 1.5 %shard_map.59 = (f32[8,128]{1,0:T(8,128)}, f32[64,128]{1,0:T(8,128)}, f32[128,128]{1,0:T(8,128)}) custom-call(f32[8,128]{1,0:T(8,128)} %get-tuple-element.9.sp, f32[64,128]{1,0:T(8,128)} %get-tuple-element.10.tp, f32[128,128]{1,0:T(8,128)} %get-tuple-element.11.mapped), custom_call_target="tpu_custom_call" | custom-call | tf_op jit(solution)/shard_map/pallas_call | solution.py:557

commit v4 on v3

--- a/solution.py
+++ b/solution.py
@@ -18,7 +18,6 @@
 ORDER = (4, 3, 5, 1, 7, 0, 2, 6)
 SIDE = 4
 WIDE = 8
-AHEAD = 2
 EARLY = 5
 
 
@@ -30,7 +29,7 @@
     src_ref, tgt_ref, pot_ref, sp_ref, tp_ref, map_ref,
     sbuf, tbuf, lhs, cols, scores, top, total, rslot, rcol,
     lsend, lrecv, call, colmax, acc, den, zsend, zland, colsum,
-    z_send, z_recv, p1_send, p2_send, sib_send, t_recv, sib_recv,
+    in_sem, z_send, z_recv, p1_send, p2_send, sib_send, t_recv, sib_recv,
     r_send, r_recv, l_send, l_recv, c_send, c_recv, m_send, m_recv,
 ):
     me = lax.axis_index("src")
@@ -65,9 +64,13 @@
     lax.fori_loop(1, NSRC, greet_src, 0)
     lax.fori_loop(1, NTGT, greet_tgt, 0)
 
+    own = [pltpu.make_async_copy(src_ref, sbuf.at[0], in_sem.at[2])]
     for h in range(2):
-        tbuf[chip, core, h] = tgt_ref[pl.ds(h * 128, 128), :]
-    sbuf[0] = src_ref[...]
+        own.append(pltpu.make_async_copy(tgt_ref.at[pl.ds(h * 128, 128)], tbuf.at[chip, core, h], in_sem.at[h]))
+    for copy in own:
+        copy.start()
+    for copy in own:
+        copy.wait()
 
     lane = lax.broadcasted_iota(jnp.int32, (128, 128), 1)
     row = lax.broadcasted_iota(jnp.int32, (128, 128), 0)
@@ -126,46 +129,41 @@
     def z_copy(n):
         up = n % 2 == 0
         sign = 1 if up else -1
-        if n < 4:
-            d, to, far = 0, (-sign * (1 + n // 2)) % NTGT, 1 + n // 2
+        second = n // 2 in (2, 4)
+        rows = pl.ds(64 if up == second else 0, 64)
+        if n < 2:
+            d, to, far, rows = 0, (-sign) % NTGT, 1, pl.ds(0, 128)
         elif n < 6:
+            d, to, far = 0, (-2 * sign) % NTGT, 2
+        elif n < 10:
             d, to, far = (-2 * sign) % NTGT, (-3 * sign) % NTGT, 1
         else:
-            rows = pl.ds(0 if up else 64, 64)
-            d = (-2 * sign) % NTGT
-            return rcopy(sbuf.at[d, rows], sbuf.at[4, rows], z_send.at[n], z_recv.at[4 if up else 8], on_tgt(z + 2 * sign))
-        return rcopy(sbuf.at[d], sbuf.at[to], z_send.at[n], z_recv.at[to], on_tgt(z + far * sign))
+            d, to, far = (-2 * sign) % NTGT, 4, 2
+        return rcopy(sbuf.at[d, rows], sbuf.at[to, rows], z_send.at[n], z_recv.at[n], on_tgt(z + far * sign))
 
     for i in range(3):
         for h in range(2):
             p1_copy(h, i).start()
-    for n in (2, 3, 0, 1):
+    for n in (2, 3, 4, 5, 0, 1):
         z_copy(n).start()
 
-    def z_wait(d):
-        rcopy(sbuf.at[d], sbuf.at[d], z_send.at[0], z_recv.at[d], on_tgt(z + 1)).wait_recv()
-
-    def z_near():
-        for d, n in ((6, 4), (2, 5)):
-            z_wait(d)
-            z_copy(n).start()
-            z_copy(n + 2).start()
-        for d in (6, 2):
+    def z_near(second):
+        for i in range(2):
+            n = 2 + 2 * second + i
+            z_copy(n).wait_recv()
+            z_copy(n + 4).start()
+            if not second:
+                z_copy(n + 8).start()
+
+    def z_late():
+        for n in (0, 1):
+            z_copy(n).wait_recv()
+        for d in (7, 1, 6, 2):
             prep_src(d)
-
-    def z_next():
-        for d in (7, 1):
-            z_wait(d)
+        for n in range(6, 12):
+            z_copy(n).wait_recv()
+        for d in (5, 3, 4):
             prep_src(d)
-
-    def z_late():
-        for d in (5, 3):
-            z_wait(d)
-            prep_src(d)
-        for i in range(2):
-            part = sbuf.at[4, pl.ds(i * 64, 64)]
-            rcopy(part, part, z_send.at[0], z_recv.at[4 + 4 * i], on_tgt(z + 1)).wait_recv()
-        prep_src(4)
 
     def place_of(m, h):
         g1 = jnp.where(m < 4, m, (m + 8) // 3 - 4)
@@ -210,53 +208,58 @@
             sib_copy(m, h, q).start()
 
     def score_rows(us, r0, n):
-        for u in us:
+        for j, u in enumerate(us):
             scores[u, pl.ds(r0, n), :] = lax.dot_general(
                 lhs[pl.ds(r0, n), :], cols[u], (((1,), (1,)), ((), ())), preferred_element_type=F32
             )
-        for r in range(r0, r0 + n, 64):
-            rows = pl.ds(r, 64)
-            parts = [scores[u, rows, pl.ds(k * 128, 128)] for u in us for k in range(2)]
-            old = top[rows, :]
-            new = old
-            for p in parts:
-                new = jnp.maximum(new, p)
-            sums = total[rows, :] * jnp.exp2(old - new)
-            for p in parts:
-                sums = sums + jnp.exp2(p - new)
-            total[rows, :] = sums
-            top[rows, :] = new
+            if j % 2 == 0:
+                continue
+            for r in range(r0, r0 + n, 64):
+                rows = pl.ds(r, 64)
+                parts = [scores[v, rows, pl.ds(k * 128, 128)] for v in (us[j - 1], u) for k in range(2)]
+                old = top[rows, :]
+                new = old
+                for p in parts:
+                    new = jnp.maximum(new, p)
+                sums = total[rows, :] * jnp.exp2(old - new)
+                for p in parts:
+                    sums = sums + jnp.exp2(p - new)
+                total[rows, :] = sums
+                top[rows, :] = new
 
     def lead(m, carry):
         gather_step(m)
 
-        @pl.when(m == 2)
-        def _():
-            z_near()
+        for n in (1, 2):
+
+            @pl.when(m == n)
+            def _():
+                z_near(n - 1)
 
         return carry
 
     lax.fori_loop(0, 4, lead, 0)
-    z_next()
     z_late()
 
-    def first_pass(p, carry):
-        m = p + AHEAD
-
-        @pl.when(jnp.logical_and(m >= 4, m < 16))
-        def _():
-            gather_step(m)
-
-        for h in range(2):
-            q = place_of(p, h)
-            piece = tbuf.at[q, 1 - core, h]
-            rcopy(piece, piece, sib_send.at[0], sib_recv.at[h * 16 + q], on_src(sib)).wait_recv()
-        for h in range(2):
-            prep_tgt(p * 2 + h, place_of(p, h), h)
-        score_rows((p * 2, p * 2 + 1), 0, EARLY * 128)
-        return carry
-
-    lax.fori_loop(0, 16, first_pass, 0)
+    def first_pass(i, carry):
+        for m in (i * 2 + 2, i * 2 + 3):
+
+            @pl.when(jnp.logical_and(m >= 4, m < 16))
+            def _():
+                gather_step(m)
+
+        for p in (i * 2, i * 2 + 1):
+            for h in range(2):
+                q = place_of(p, h)
+                piece = tbuf.at[q, 1 - core, h]
+                rcopy(piece, piece, sib_send.at[0], sib_recv.at[h * 16 + q], on_src(sib)).wait_recv()
+        for p in (i * 2, i * 2 + 1):
+            for h in range(2):
+                prep_tgt(p * 2 + h, place_of(p, h), h)
+        score_rows([i * 4 + j for j in range(4)], 0, EARLY * 128)
+        return carry
+
+    lax.fori_loop(0, 8, first_pass, 0)
 
     def r_copy(part, i):
         slot = rslot.at[part, z]
@@ -296,31 +299,12 @@
     row_sums(0, early)
 
     def late_rows(i, carry):
-        score_rows([i * 4 + j for j in range(4)], EARLY * 128, 1024 - EARLY * 128)
-        return carry
-
-    lax.fori_loop(0, 8, late_rows, 0)
+        score_rows([i * 8 + j for j in range(8)], EARLY * 128, 1024 - EARLY * 128)
+        return carry
+
+    lax.fori_loop(0, 4, late_rows, 0)
     row_sums(1, late)
 
-    for h in range(2):
-        for i in range(3):
-            p1_copy(h, i).wait_send()
-    for n in range(8):
-        z_copy(n).wait_send()
-
-    def gather_sent(m, carry):
-        for h in range(2):
-            q = place_of(m, h)
-
-            @pl.when(m < 4)
-            def _():
-                for i in range(3):
-                    p2_copy(m, h, q, i).wait_send()
-
-            sib_copy(m, h, q).wait_send()
-        return carry
-
-    lax.fori_loop(0, 16, gather_sent, 0)
     row_totals(0, early)
 
     def l_copy(u):
@@ -345,24 +329,29 @@
             colmax[slot, pl.ds(b0, n), lanes] = jnp.concatenate(tops, axis=0)
             colsum[slot, pl.ds(b0, n), lanes] = jnp.concatenate(sums, axis=0)
 
-    def early_blocks(slot, carry):
-        column_blocks(slot, early)
-        return carry
-
-    def late_blocks(u, carry):
-        slot = slot_of(u)
-        column_blocks(slot, late)
-        tops = colmax[slot]
-        high = jnp.max(tops, axis=0, keepdims=True)
-        lsend[u] = high + jnp.log2(jnp.sum(colsum[slot] * jnp.exp2(tops - high), axis=0, keepdims=True))
-
-        @pl.when(u != me)
-        def _():
-            l_copy(u).start()
-
-        @pl.when(u == me)
-        def _():
-            lrecv[me] = lsend[u]
+    def early_blocks(i, carry):
+        for j in range(4):
+            column_blocks(i * 4 + j, early)
+        return carry
+
+    def late_blocks(i, carry):
+        us = (2 * i, 2 * i + 1)
+        slots = [slot_of(u) for u in us]
+        for slot in slots:
+            column_blocks(slot, late)
+        for u, slot in zip(us, slots):
+            tops = colmax[slot]
+            high = jnp.max(tops, axis=0, keepdims=True)
+            lsend[u] = high + jnp.log2(jnp.sum(colsum[slot] * jnp.exp2(tops - high), axis=0, keepdims=True))
+        for u in us:
+
+            @pl.when(u != me)
+            def _():
+                l_copy(u).start()
+
+            @pl.when(u == me)
+            def _():
+                lrecv[me] = lsend[u]
 
         return carry
 
@@ -384,9 +373,29 @@
 
         lax.fori_loop(1, NSRC, tell, 0)
 
-    lax.fori_loop(0, NSRC, early_blocks, 0)
+    lax.fori_loop(0, NSRC // 4, early_blocks, 0)
     row_totals(1, late)
-    lax.fori_loop(0, NSRC, late_blocks, 0)
+    lax.fori_loop(0, NSRC // 2, late_blocks, 0)
+
+    for h in range(2):
+        for i in range(3):
+            p1_copy(h, i).wait_send()
+    for n in range(12):
+        z_copy(n).wait_send()
+
+    def gather_sent(m, carry):
+        for h in range(2):
+            q = place_of(m, h)
+
+            @pl.when(m < 4)
+            def _():
+                for i in range(3):
+                    p2_copy(m, h, q, i).wait_send()
+
+            sib_copy(m, h, q).wait_send()
+        return carry
+
+    lax.fori_loop(0, 16, gather_sent, 0)
     column_total()
 
     acc[...] = jnp.zeros((1024, 256), F32)
@@ -510,7 +519,7 @@
     results = pl.pallas_call(
         kernel,
         out_shape=shapes,
-        in_specs=[vmem] * 3,
+        in_specs=[pl.BlockSpec(memory_space=pl.ANY)] * 2 + [vmem],
         out_specs=(vmem,) * 3,
         scratch_shapes=[
             pltpu.VMEM((8, 128, 128), F32),
@@ -531,8 +540,9 @@
             pltpu.VMEM((8, 136, 128), F32),
             pltpu.VMEM((8, 136, 128), F32),
             pltpu.VMEM((32, 8, 256), F32),
-            dma((8,)),
-            dma((9,)),
+            dma((3,)),
+            dma((12,)),
+            dma((16,)),
             dma((6,)),
             dma((24,)),
             dma((32,)),

time: 83 us -> 77.6 us (0.935)
  Pallas kernels: 82.2 us -> 76.7 us
    pallas_call x1, Pallas kernels: 80.7 us -> 75.2 us  [per_device(): pl.pallas_call(kernel, out_shape=shapes, in_specs=[pl.BlockSpec(memory_sp...]
where the time goes in v4:
time: 77.6 us; the launch traced here: 77.4 us
  Pallas kernels  76.7 us (99%)
    pallas_call x1, Pallas kernels, per_device(): pl.pallas_call(kernel, out_shape=shapes, in_specs=[pl.BlockSpec(memory_sp...  75.2 us

profile of v4, /device:TPU:1, one launch (start us, length us, event | category | flops | bytes accessed | tf_op | source)
XLA Modules:
  0.0 77.4 jit_solution(13724022630749406528)
XLA Ops:
  0.6 75.2 %shard_map.58 = (f32[8,128]{1,0:T(8,128)}, f32[64,128]{1,0:T(8,128)}, f32[128,128]{1,0:T(8,128)}) custom-call(f32[128,128]{1,0:T(8,128)} %src_ref.1, f32[256,128]{1,0:T(8,128)} %tgt_ref.1, f32[64,128]{1,0:T(8,128)} %bitcast.3), custom_call_target="tpu_custom_call" | custom-call | flops 17179869184 | bytes 1048576 | tf_op jit(solution)/shard_map/pallas_call | solution.py:519
  75.8 1.5 %shard_map.59 = (f32[8,128]{1,0:T(8,128)}, f32[64,128]{1,0:T(8,128)}, f32[128,128]{1,0:T(8,128)}) custom-call(f32[8,128]{1,0:T(8,128)} %get-tuple-element.9.sp, f32[64,128]{1,0:T(8,128)} %get-tuple-element.10.tp, f32[128,128]{1,0:T(8,128)} %get-tuple-element.11.mapped), custom_call_target="tpu_custom_call" | custom-call | tf_op jit(solution)/shard_map/pallas_call | solution.py:567

commit v5 on v4

--- a/solution.py
+++ b/solution.py
@@ -15,7 +15,7 @@
 BF16 = jnp.bfloat16
 NSRC = 32
 NTGT = 8
-ORDER = (4, 3, 5, 1, 7, 0, 2, 6)
+ORDER = (4, 3, 5, 1, 7, 2, 6, 0)
 SIDE = 4
 WIDE = 8
 EARLY = 5
@@ -460,11 +460,11 @@
     for n, d in ((0, 4), (1, 4), (2, 3), (3, 5)):
         put(n, ORDER.index(d))
         z_sum(n).start()
-    map_rows(ORDER[3:6], False)
+    map_rows(ORDER[3:5], False)
     for n, d in ((6, 1), (7, 7)):
         put(n, ORDER.index(d))
         z_sum(n).start()
-    map_rows(ORDER[6:8], False)
+    map_rows(ORDER[5:7], False)
     for n, d in ((4, 2), (5, 6)):
         put(n, ORDER.index(d))
         for k in (n - 4, n - 2):
@@ -473,6 +473,7 @@
         part = pl.ds(0, 64) if n == 4 else pl.ds(64, 72)
         zsend[n, part, :] += zland[n - 4, part, :]
         z_sum(n).start()
+    map_rows(ORDER[7:8], False)
     own_num, own_den = block(ORDER.index(0))
 
     for u in range(NSRC):

time: 77.6 us -> 76.4 us (0.985)
  Pallas kernels: 76.7 us -> 75.5 us
    pallas_call x1, Pallas kernels: 75.2 us -> 74 us  [per_device(): pl.pallas_call(kernel, out_shape=shapes, in_specs=[pl.BlockSpec(memory_sp...]
where the time goes in v5:
time: 76.4 us; the launch traced here: 76.1 us
  Pallas kernels  75.5 us (99%)
    pallas_call x1, Pallas kernels, per_device(): pl.pallas_call(kernel, out_shape=shapes, in_specs=[pl.BlockSpec(memory_sp...  74 us

profile of v5, /device:TPU:1, one launch (start us, length us, event | category | flops | bytes accessed | tf_op | source)
XLA Modules:
  0.0 76.1 jit_solution(5549709885635390326)
XLA Ops:
  0.6 74.0 %shard_map.58 = (f32[8,128]{1,0:T(8,128)}, f32[64,128]{1,0:T(8,128)}, f32[128,128]{1,0:T(8,128)}) custom-call(f32[128,128]{1,0:T(8,128)} %src_ref.1, f32[256,128]{1,0:T(8,128)} %tgt_ref.1, f32[64,128]{1,0:T(8,128)} %bitcast.3), custom_call_target="tpu_custom_call" | custom-call | flops 17179869184 | bytes 1048576 | tf_op jit(solution)/shard_map/pallas_call | solution.py:520
  74.6 1.5 %shard_map.59 = (f32[8,128]{1,0:T(8,128)}, f32[64,128]{1,0:T(8,128)}, f32[128,128]{1,0:T(8,128)}) custom-call(f32[8,128]{1,0:T(8,128)} %get-tuple-element.9.sp, f32[64,128]{1,0:T(8,128)} %get-tuple-element.10.tp, f32[128,128]{1,0:T(8,128)} %get-tuple-element.11.mapped), custom_call_target="tpu_custom_call" | custom-call | tf_op jit(solution)/shard_map/pallas_call | solution.py:568

commit v6 on v5

--- a/solution.py
+++ b/solution.py
@@ -308,7 +308,7 @@
     row_totals(0, early)
 
     def l_copy(u):
-        return rcopy(lsend.at[u], lrecv.at[me], l_send.at[u], l_recv.at[me], on_src(u))
+        return rcopy(lsend.at[u], lrecv.at[me], l_send.at[u], l_recv.at[0], on_src(u))
 
     def c_copy(i):
         return rcopy(call.at[me], call.at[me], c_send.at[i], c_recv.at[me], on_src((me + i) % NSRC))
@@ -356,13 +356,8 @@
         return carry
 
     def column_total():
-        def arrived(i, carry):
-            other = (me + i) % NSRC
-            slot = lrecv.at[other]
-            rcopy(slot, slot, l_send.at[0], l_recv.at[other], on_src(other)).wait_recv()
-            return carry
-
-        lax.fori_loop(1, NSRC, arrived, 0)
+        others = lrecv.at[pl.ds(0, NSRC - 1)]
+        rcopy(others, others, l_send.at[0], l_recv.at[0], on_src(sib)).wait_recv()
         parts = lrecv[...]
         high = jnp.max(parts, axis=0)
         call[me] = high + jnp.log2(jnp.sum(jnp.exp2(parts - high[None]), axis=0))
@@ -552,7 +547,7 @@
             dma((16,)),
             dma((16,)),
             dma((32,)),
-            dma((32,)),
+            dma((1,)),
             dma((32,)),
             dma((32,)),
             dma((8,)),

time: 76.4 us -> 75.9 us (level)
  no operation moved by 1% of the time
where the time goes in v6:
time: 75.9 us; the launch traced here: 75.7 us
  Pallas kernels  75 us (99%)
    pallas_call x1, Pallas kernels, per_device(): pl.pallas_call(kernel, out_shape=shapes, in_specs=[pl.BlockSpec(memory_sp...  73.5 us

profile of v6, /device:TPU:1, one launch (start us, length us, event | category | flops | bytes accessed | tf_op | source)
XLA Modules:
  0.0 75.7 jit_solution(3065851088430800452)
XLA Ops:
  0.6 73.5 %shard_map.58 = (f32[8,128]{1,0:T(8,128)}, f32[64,128]{1,0:T(8,128)}, f32[128,128]{1,0:T(8,128)}) custom-call(f32[128,128]{1,0:T(8,128)} %src_ref.1, f32[256,128]{1,0:T(8,128)} %tgt_ref.1, f32[64,128]{1,0:T(8,128)} %bitcast.3), custom_call_target="tpu_custom_call" | custom-call | flops 17179869184 | bytes 1048576 | tf_op jit(solution)/shard_map/pallas_call | solution.py:515
  74.2 1.5 %shard_map.59 = (f32[8,128]{1,0:T(8,128)}, f32[64,128]{1,0:T(8,128)}, f32[128,128]{1,0:T(8,128)}) custom-call(f32[8,128]{1,0:T(8,128)} %get-tuple-element.9.sp, f32[64,128]{1,0:T(8,128)} %get-tuple-element.10.tp, f32[128,128]{1,0:T(8,128)} %get-tuple-element.11.mapped), custom_call_target="tpu_custom_call" | custom-call | tf_op jit(solution)/shard_map/pallas_call | solution.py:563
